TPU v7x, 512 devices: a whole 4x8x8 slice. The times are simulated.
512 devices in a mesh: row: 16 (over y, core), col: 32 (over z, x).
Axes of the slice: x: 4, y: 8, z: 8, core: 2. Of those that a mesh axis runs over, the one named last changes fastest.
Arguments:
- hessian: float32 [6, 16, 128, 3, 32, 128], P(None, 'row', None, None, 'col'), may hold values from -4 to 9, as said below
Outputs:
- reduced: float32 [6, 16, 128, 3, 32, 128], P(None, 'row', None, None, 'col')
Inputs may be any that keep to these rules, and one draw needn't show every extreme that they name: hessian is symmetric as a 12288 x 12288 matrix A, and for every j < 64 the entry A[64 + j, j] is at least twice the Euclidean norm of the other entries of column j in rows 64 and below.
All inputs are finite; a program needn't handle non-finite values.
Results may differ from a plain program's by a relative error of at most 0.0001.
Values sent between devices are 32-bit elements; how exact they have to be, the bound alone decides.
A program may use at most 64 MiB of HBM per device.

v0:
```python
import jax
import jax.numpy as jnp
from jax import lax
from jax.sharding import PartitionSpec as P

NB = 64


highest = lax.Precision.HIGHEST


def broadcast(block, axis, owner):
    block = jnp.where(lax.axis_index(axis) == owner, block, jnp.zeros_like(block))
    return lax.psum(block, axis)


def matmul(left, right):
    return jnp.dot(left, right, precision=highest, preferred_element_type=jnp.float32)


def contract(left, right):
    return lax.dot_general(
        left, right, (((0,), (0,)), ((), ())), precision=highest, preferred_element_type=jnp.float32
    )


def outer_product(left, right):
    return lax.dot_general(
        left, right, (((1,), (1,)), ((), ())), precision=highest, preferred_element_type=jnp.float32
    )


def lower_inverse(lower, unit):
    positions = jnp.arange(NB)

    def substitute(step, inverse):
        lower_row = lax.dynamic_index_in_dim(lower, step, 0, keepdims=False)
        unit_row = (positions == step).astype(jnp.float32)
        new_row = unit_row - matmul(lower_row, inverse)
        if not unit:
            new_row = new_row / lower_row[step]
        return lax.dynamic_update_index_in_dim(inverse, new_row, step, 0)

    return lax.fori_loop(0, NB, substitute, jnp.zeros((NB, NB), jnp.float32))


def upper_inverse(upper):
    return lower_inverse(upper.T, False).T


def cholesky_lower(gram_matrix):
    positions = jnp.arange(NB)

    def advance(step, factor_lower):
        factor_row = lax.dynamic_index_in_dim(factor_lower, step, 0, keepdims=False)
        gram_column = lax.dynamic_index_in_dim(gram_matrix, step, 1, keepdims=False)
        remaining = gram_column - matmul(factor_lower, factor_row)
        pivot_root = jnp.sqrt(remaining[step])
        column = jnp.where(
            positions > step, remaining / pivot_root, jnp.where(positions == step, pivot_root, 0.0)
        )
        return lax.dynamic_update_index_in_dim(factor_lower, column, step, 1)

    return lax.fori_loop(0, NB, advance, jnp.zeros((NB, NB), jnp.float32))


def unpivoted_lu(matrix):
    positions = jnp.arange(NB)

    def eliminate(step, current):
        pivot_value = current[step, step]
        multipliers = jnp.where(positions > step, current[:, step] / pivot_value, 0.0)
        pivot_row = jnp.where(positions > step, current[step, :], 0.0)
        current = current - multipliers[:, None] * pivot_row[None, :]
        return current.at[:, step].set(jnp.where(positions > step, multipliers, current[:, step]))

    packed = lax.fori_loop(0, NB, eliminate, matrix)
    unit_lower = jnp.tril(packed, -1) + jnp.eye(NB, dtype=jnp.float32)
    return (unit_lower, jnp.triu(packed))


def gram_factor(work_rows, work_global, pivot_block):
    gram_matrix = lax.psum(contract(work_rows, work_rows), "row")
    identity = jnp.eye(NB, dtype=jnp.float32)
    factor_lower = cholesky_lower(gram_matrix)
    inverse_lower = lower_inverse(factor_lower, False)
    orthonormal = matmul(work_rows, inverse_lower.T)
    leading = matmul(pivot_block, inverse_lower.T)
    unit_lower, upper = unpivoted_lu(leading + identity)
    inverse_upper = upper_inverse(upper)
    remainder = matmul(orthonormal, inverse_upper)
    selector = (work_global[:, None] - NB == jnp.arange(NB)[None, :]).astype(jnp.float32)
    reflectors = jnp.where(work_global[:, None] >= 2 * NB, remainder, matmul(selector, unit_lower))
    inverse_unit = lower_inverse(unit_lower, True)
    block_factor = matmul(upper, inverse_unit.T)
    return (reflectors, block_factor)


def own_tiles(rows_array, col_index, row_count, col_tiles, tile_size):
    grouped = rows_array.reshape(col_tiles, -1, tile_size, NB)
    picked = lax.dynamic_index_in_dim(grouped, col_index // row_count, 1, keepdims=False)
    return picked.reshape(-1, NB)


def body(hessian):
    row_tiles = hessian.shape[0]
    tile_size = hessian.shape[2]
    col_tiles = hessian.shape[3]
    row_count = lax.axis_size("row")
    row_index = lax.axis_index("row")
    col_index = lax.axis_index("col")
    local_block = hessian.reshape(row_tiles * tile_size, col_tiles * tile_size)
    offsets = jnp.arange(tile_size)
    row_global = (
        (jnp.arange(row_tiles)[:, None] * row_count + row_index) * tile_size + offsets[None, :]
    ).reshape(-1)
    panel_rows = broadcast(local_block[:, :NB], "col", 0)
    panel_rows = jnp.where(row_global[:, None] >= NB, panel_rows, 0.0)
    pivot_block = broadcast(panel_rows[NB : 2 * NB], "row", 0)
    reflectors, block_factor = gram_factor(panel_rows, row_global, pivot_block)
    owner_row = col_index % row_count
    col_reflectors = broadcast(
        own_tiles(reflectors, col_index, row_count, col_tiles, tile_size), "row", owner_row
    )
    image_rows = lax.psum(matmul(local_block, col_reflectors), "col")
    curvature = lax.psum(contract(reflectors, image_rows), "row")
    cross = matmul(matmul(block_factor.T, curvature), block_factor)
    update_rows = matmul(image_rows, block_factor) - 0.5 * matmul(reflectors, cross)
    update_cols = broadcast(
        own_tiles(update_rows, col_index, row_count, col_tiles, tile_size), "row", owner_row
    )
    reduced = (
        local_block
        - outer_product(update_rows, col_reflectors)
        - outer_product(reflectors, update_cols)
    )
    return reduced.reshape(hessian.shape)


def solution(mesh):
    return jax.shard_map(
        body,
        mesh=mesh,
        in_specs=(P(None, "row", None, None, "col", None),),
        out_specs=P(None, "row", None, None, "col", None),
        check_vma=False,
    )
```

profile of v0, /device:TPU:1, one launch (start us, length us, event | category | flops | bytes accessed | tf_op | source)
XLA Modules:
  0.0 1185.4 jit_solution(8819419056337610907)
XLA Ops:
  6.5 4.5 reduce.11
  12.2 157.9 %all-reduce.6.cloned.1.call-done = f32[768,64]{1,0:T(8,128)} async-done(((f32[768,64]{1,0:T(8,128)}), f32[768,64]{1,0:T(8,128)}) %all-reduce.6.cloned.1.call-update) | async-done | bytes 196624 | tf_op jit(solution)/shard_map/psum | solution.py:14
  172.0 47.4 %all-reduce = (f32[64,64]{1,0:T(8,128)S(1)}, f32[64,64]{1,0:T(8,128)S(1)}) all-reduce(f32[64,64]{1,0:T(8,128)S(1)} %fusion.48, f32[64,64]{1,0:T(8,128)S(1)} %slice_select_fusion.1), channel_id=1, replica_groups=mesh['row'=16,'col'=32] {'row'}, use_global_device_ids=true, to_apply=%region_1.2 | all-reduce | flops 8192 | bytes 65536 | tf_op jit(solution)/shard_map/psum | solution.py:83
  219.5 114.9 %while.82 = (s32[]{:T(128)}, f32[64,64]{1,0:T(8,128)S(1)}, f32[64,64]{0,1:T(8,128)S(1)}, s32[]{:T(128)}, s32[]{:T(128)}) while((s32[]{:T(128)}, f32[64,64]{1,0:T(8,128)S(1)}, f32[64,64]{0,1:T(8,128)S(1)}, s32[]{:T(128)}, s32[]{:T(128)}) %tuple.176), condition=%wide.region_3.4_spmd.clone.clone, body=%wide.region_2.3_spmd.clone.clone.sunk | while | flops 49538 | bytes 36701 | solution.py:64
  334.4 90.5 %while.78 = (s32[]{:T(128)}, f32[64,64]{1,0:T(8,128)S(1)}, f32[64,64]{1,0:T(8,128)S(1)}, s32[]{:T(128)}, s32[]{:T(128)}, /*index=5*/s32[]{:T(128)}) while((s32[]{:T(128)}, f32[64,64]{1,0:T(8,128)S(1)}, f32[64,64]{1,0:T(8,128)S(1)}, s32[]{:T(128)}, s32[]{:T(128)}, /*index=5*/s32[]{:T(128)}) %tuple.179), condition=%wide.region_5.6_spmd.clone, body=%wide.region_4.5_spmd.clone.sunk | while | flops 49411 | bytes 35685 | solution.py:44
  425.7 232.3 %while.79 = (s32[]{:T(128)}, f32[64,64]{0,1:T(8,128)S(1)}, s32[]{:T(128)}, s32[1]{0:T(128)}, s32[]{:T(128)}) while((s32[]{:T(128)}, f32[64,64]{0,1:T(8,128)S(1)}, s32[]{:T(128)}, s32[1]{0:T(128)}, s32[]{:T(128)}) %tuple.182), condition=%wide.region_9.10_spmd.clone, body=%wide.region_7.9_spmd.clone.sunk | while | flops 8845 | bytes 105814 | solution.py:77
  431.5 1.3 broadcast_select_fusion.5
  435.2 1.3 broadcast_select_fusion.5
  442.4 1.3 broadcast_select_fusion.5
  446.0 1.3 broadcast_select_fusion.5
  449.7 1.3 broadcast_select_fusion.5
  453.3 1.3 broadcast_select_fusion.5
  456.9 1.3 broadcast_select_fusion.5
  460.6 1.3 broadcast_select_fusion.5
  464.2 1.3 broadcast_select_fusion.5
  471.4 1.3 broadcast_select_fusion.5
  475.1 1.3 broadcast_select_fusion.5
  482.3 1.3 broadcast_select_fusion.5
  486.0 1.3 broadcast_select_fusion.5
  489.6 1.3 broadcast_select_fusion.5
  493.2 1.3 broadcast_select_fusion.5
  500.5 1.3 broadcast_select_fusion.5
  504.1 1.3 broadcast_select_fusion.5
  511.4 1.3 broadcast_select_fusion.5
  515.0 1.3 broadcast_select_fusion.5
  518.6 1.3 broadcast_select_fusion.5
  522.2 1.3 broadcast_select_fusion.5
  525.9 1.3 broadcast_select_fusion.5
  529.5 1.3 broadcast_select_fusion.5
  533.1 1.3 broadcast_select_fusion.5
  540.4 1.3 broadcast_select_fusion.5
  544.0 1.3 broadcast_select_fusion.5
  551.3 1.3 broadcast_select_fusion.5
  554.9 1.3 broadcast_select_fusion.5
  558.5 1.3 broadcast_select_fusion.5
  562.2 1.3 broadcast_select_fusion.5
  569.4 1.3 broadcast_select_fusion.5
  573.1 1.3 broadcast_select_fusion.5
  580.3 1.3 broadcast_select_fusion.5
  658.2 90.5 %while.80 = (s32[]{:T(128)}, f32[64,64]{1,0:T(8,128)S(1)}, f32[64,64]{1,0:T(8,128)S(1)}, s32[]{:T(128)}, s32[]{:T(128)}, /*index=5*/s32[]{:T(128)}) while((s32[]{:T(128)}, f32[64,64]{1,0:T(8,128)S(1)}, f32[64,64]{1,0:T(8,128)S(1)}, s32[]{:T(128)}, s32[]{:T(128)}, /*index=5*/s32[]{:T(128)}) %tuple.185), condition=%wide.region_11.12_spmd.clone, body=%wide.region_10.11_spmd.clone.sunk | while | flops 49411 | bytes 35685 | solution.py:44
  751.0 11.5 while.81
  762.5 97.8 %all-reduce.8.cloned.1.call-done = f32[384,64]{0,1:T(8,128)} async-done(((f32[384,64]{0,1:T(8,128)}), f32[384,64]{0,1:T(8,128)}) %all-reduce.8.cloned.1.call-update) | async-done | bytes 98320 | tf_op jit(solution)/shard_map/psum | solution.py:14
  860.3 2.8 convolution_bitcast_fusion.4
  863.4 149.9 %all-reduce.10.cloned.1.call-done = f32[768,64]{0,1:T(8,128)} async-done(((f32[768,64]{0,1:T(8,128)}), f32[768,64]{0,1:T(8,128)}) %all-reduce.10.cloned.1.call-update) | async-done | bytes 196624 | tf_op jit(solution)/shard_map/psum | solution.py:125
  1014.5 47.5 %psum.54 = f32[64,64]{1,0:T(8,128)S(1)} all-reduce(f32[64,64]{1,0:T(8,128)S(1)} %fusion.52), channel_id=1, replica_groups=mesh['row'=16,'col'=32] {'row'}, use_global_device_ids=true, to_apply=%region_16.17 | all-reduce | flops 4096 | bytes 32768 | tf_op jit(solution)/shard_map/psum | solution.py:126
  1066.4 108.2 %all-reduce.12.cloned.1.call-done = f32[384,64]{0,1:T(8,128)} async-done(((f32[384,64]{0,1:T(8,128)}), f32[384,64]{0,1:T(8,128)}) %all-reduce.12.cloned.1.call-update) | async-done | bytes 98320 | tf_op jit(solution)/shard_map/psum | solution.py:14
  1174.6 2.0 convolution_subtract_fusion
  1176.7 2.2 reshape.164
  (1420 shorter events, 454.6 us)
Async XLA Ops:
  6.5 163.5 %all-reduce.6.cloned.1.call-start = ((), (), s32[]{:S(2)}) async-start(), calls=%async_computation | async-start | bytes 786432 | tf_op jit(solution)/shard_map/psum | solution.py:14
  11.9 848.3 %all-reduce.8.cloned.1.call-start = ((), (), s32[]{:S(2)}) async-start(), calls=%async_computation.1 | async-start | bytes 196608 | tf_op jit(solution)/shard_map/psum | solution.py:14
  750.9 262.4 %all-reduce.10.cloned.1.call-start = ((), (), s32[]{:S(2)}) async-start(), calls=%async_computation.2 | async-start | bytes 393216 | tf_op jit(solution)/shard_map/psum | solution.py:125
  863.1 311.5 %all-reduce.12.cloned.1.call-start = ((), (), s32[]{:S(2)}) async-start(), calls=%async_computation.3 | async-start | bytes 196608 | tf_op jit(solution)/shard_map/psum | solution.py:14
  1014.5 50.7 %copy-start = (f32[384,64]{0,1:T(8,128)S(1)}, f32[384,64]{0,1:T(8,128)}, u32[]{:S(2)}) copy-start(f32[384,64]{0,1:T(8,128)} %all-reduce.8.cloned.1.call-done) | copy-start | bytes 294916
Sparse Core Ops, SparseCore 0:
  12.0 157.9 all-reduce.5
  751.0 109.1 all-reduce.7
  863.7 149.5 all-reduce.9
  1065.4 109.1 all-reduce.11
where the time goes:
time: 1190 us
  waiting for transfers between devices  514 us (43%)
  other arithmetic  192 us (16%)
  local copies, waits for them, and re-layouts  189 us (16%)
  matrix products  130 us (11%)
  blocking collectives  94.9 us (8%)
  loops' own time  52.8 us (4%)
  between operations  13.4 us (1%)
    psum x3, waiting for transfers between devices, broadcast(): return lax.psum(block, axis)  364 us
    psum x1, waiting for transfers between devices, body(): image_rows = lax.psum(matmul(local_block, col_reflectors), 'col')  150 us
    another operation x128, other arithmetic  137 us
    dot_general x266, matrix products, matmul(): jnp.dot(left, right, precision=highest, preferred_element_type=jnp.float32)  125 us
    dynamic_slice x128, local copies, waits for them, and re-layouts, substitute(): new_row = new_row / lower_row[step]  75.3 us
    psum x1, blocking collectives, body(): curvature = lax.psum(contract(reflectors, image_rows), 'row')  47.5 us
    psum x1, blocking collectives, gram_factor(): gram_matrix = lax.psum(contract(work_rows, work_rows), 'row')  47.4 us
    another operation x1, loops' own time, cholesky_lower(): return lax.fori_loop(0, NB, advance, jnp.zeros((NB, NB), jnp.float32))  46.3 us
  transfers between devices with their start and end apart: 4, of which 4 were waited for; matrix products, arithmetic and copies ran while one was open for 1% of the time, Pallas kernels for 0%

commit v1 on v0

v1 whole, which is shorter than its diff:
```python
import functools

import jax
import jax.numpy as jnp
from jax import lax
from jax.experimental import pallas as pl
from jax.experimental.pallas import tpu as pltpu
from jax.sharding import PartitionSpec as P

NB = 64
MESH = pl.DeviceIdType.MESH
HIGHEST = lax.Precision.HIGHEST
F32 = jnp.float32


def dot_nn(a, b):
    return lax.dot_general(a, b, (((1,), (0,)), ((), ())), precision=HIGHEST, preferred_element_type=F32)


def dot_nt(a, b):
    return lax.dot_general(a, b, (((1,), (1,)), ((), ())), precision=HIGHEST, preferred_element_type=F32)


def spiral(q, n):
    return lax.rem(n // 2 + (1 - 2 * lax.rem(q, 2)) * lax.div(q + 1, 2), n)


def loop(lo, hi, f):
    def step(i, carry):
        f(i)
        return carry

    lax.fori_loop(lo, hi, step, 0)


def factor_cholesky(g, ct):
    lane1 = lax.broadcasted_iota(jnp.int32, (1, 128), 1)
    for k in range(NB):
        col = g[:, k : k + 1]
        row = g[k : k + 1, :]
        piv = g[k : k + 1, k : k + 1]
        ct[NB + k : NB + k + 1, :] = jnp.where((lane1 >= k) & (lane1 < NB), row * lax.rsqrt(piv), 0.0)
        if k < NB - 1:
            low = (k + 1) // 8 * 8
            part = g[low:, :] - col[low:, :] * (row / piv)
            g = part if low == 0 else jnp.concatenate([g[:low, :], part], axis=0)


def invert(m):
    lane1 = lax.broadcasted_iota(jnp.int32, (1, 128), 1)
    lane = lax.broadcasted_iota(jnp.int32, (NB, 128), 1)
    sub = lax.broadcasted_iota(jnp.int32, (NB, 128), 0)
    for k in range(NB):
        col = m[:, k : k + 1]
        row = m[k : k + 1, :]
        piv = m[k : k + 1, k : k + 1]
        scaled = jnp.where(lane1 == k, 1.0, row) / piv
        m = jnp.where(sub == k, scaled, jnp.where(lane == k, 0.0, m) - col * scaled)
    return m


def kernel(
    a_hbm, o_hbm, a_v, colpb, rowpb, zpart, zrecv, zrows, zcols, gpk, grecv, gfin, p1, hsend, hrecv, hall, ct, c0, om,
    local_sem, out_sem, colp_s, colp_r, fwd_s, sc_s, sc_r, ag_s, ag_r, rs_s, rs_r, zr_s, zr_r, zc_s, zc_r,
    g_s, g_r, gb_s, gb_r, p1_s, p1_r, h_s, h_r, ha_s, ha_r, c0_s, c0_r,
):
    r, c = lax.axis_index("row"), lax.axis_index("col")
    y, core = lax.div(r, 2), lax.rem(r, 2)
    z, x = lax.div(c, 4), lax.rem(c, 4)
    zodd = lax.rem(z, 2)
    mine = lax.div(c, 2)
    owner = lax.rem(x + z, 2) == 0
    my_g, my_h = lax.rem(mine, 8), lax.div(mine, 8)
    partner = c + 1 - 2 * lax.rem(c, 2)
    home = lax.rem(c, 16) == r
    lane = lax.broadcasted_iota(jnp.int32, (NB, 128), 1)

    def panel_owner(k):
        return 2 * k + lax.rem(lax.div(k, 2), 2)

    def col_peer(p):
        return lax.rem(z + spiral(lax.div(p, 4), 8), 8) * 4 + lax.rem(x + spiral(lax.rem(p, 4), 4), 4)

    def row_peer(p):
        return lax.rem(y + spiral(lax.div(p, 2), 8), 8) * 2 + lax.rem(core + 1 - lax.rem(p, 2), 2)

    def copy(src, dst, ssem, rsem, dev):
        return pltpu.make_async_remote_copy(
            src_ref=src, dst_ref=dst, send_sem=ssem, recv_sem=rsem, device_id=dev, device_id_type=MESH
        )

    def chunk(k, part):
        rows = pl.multiple_of(lax.rem(k, 8) * 8 + part * NB, 8)
        return rowpb.at[lax.div(k, 8), :, pl.ds(rows, 8), :]

    load = pltpu.make_async_copy(a_hbm, a_v, local_sem)
    load.start()
    barrier = pltpu.get_barrier_semaphore()

    def greet(dev):
        pl.semaphore_signal(barrier, inc=1, device_id=dev, device_id_type=MESH)

    loop(0, 31, lambda p: greet((r, col_peer(p))))
    loop(0, 15, lambda p: greet((row_peer(p), c)))

    @pl.when(jnp.logical_not(home))
    def _():
        loop(0, 8, lambda g: greet((lax.rem(c, 16), panel_owner(g + 8 * lax.div(c, 16)))))

    load.wait()

    def panel_cols(ref, s):
        return jnp.where((c == 0) & (s == 0) & (lane < NB), 0.0, ref[pl.ds(s, NB, stride=3), :])

    @pl.when(c == 0)
    def _():
        full = lax.broadcasted_iota(jnp.int32, (128, 128), 0)
        fulll = lax.broadcasted_iota(jnp.int32, (128, 128), 1)
        for t in range(6):
            block = jnp.transpose(a_v[pl.ds(t * 384, 128, stride=3), :])
            if t == 0:
                block = jnp.where((r == 0) & (full < NB) & (fulll < NB), 0.0, block)
            rowpb[t % 2, t // 2] = block

    @pl.when(r == 0)
    def _():
        panel = jnp.concatenate([panel_cols(a_v, s) for s in range(3)], axis=1)
        zero = jnp.zeros_like(panel)
        gpk[...] = dot_nt(panel[:32], jnp.concatenate([panel, zero], axis=0)) + dot_nt(
            panel[32:], jnp.concatenate([zero, panel], axis=0)
        )

    @pl.when(owner)
    def _():
        pl.semaphore_wait(barrier, 61)

    @pl.when(jnp.logical_not(owner))
    def _():
        pl.semaphore_wait(barrier, 46)

    def send_col(part):
        rows = pl.ds(192 * part, 192)

        def to(q):
            other = 2 * spiral(q, 8) + jnp.where(q == 7, 1, 0)
            copy(a_v.at[rows], colpb.at[rows], colp_s.at[part * 8 + q], colp_r.at[part], (other, c)).start()

        loop(0, 8, to)

    def wait_col(part):
        rows = pl.ds(192 * part, 192)

        @pl.when(r == 0)
        def _():
            colpb[rows, :] = a_v[rows, :]

        @pl.when(r != 0)
        def _():
            copy(a_v.at[rows], colpb.at[rows], colp_s.at[0], colp_r.at[part], (0, c)).wait_recv()

            @pl.when(core == 0)
            def _():
                copy(colpb.at[rows], colpb.at[rows], fwd_s.at[part], colp_r.at[part], (r + 1, c)).start()

    def scatter(part):
        def to(k):
            dev = panel_owner(k) if part == 0 else 4 * lax.div(k, 2) * 1 + 2 * lax.rem(k, 2) + 1 - lax.rem(lax.div(k, 2), 2)
            copy(chunk(k, part), chunk(k, part), sc_s.at[part * 16 + k], sc_r, (r, dev)).start()

        loop(1 - part, 16, to)

    @pl.when(r == 0)
    def _():
        send_col(0)

    @pl.when(c == 0)
    def _():
        scatter(0)

    @pl.when(r == 0)
    def _():
        grecv[c] = gpk[...]
        loop(0, 31, lambda p: copy(gpk, grecv.at[c], g_s.at[p], g_r.at[c], (r, col_peer(p))).start())

    @pl.when(c == 0)
    def _():
        scatter(1)

    @pl.when(r == 0)
    def _():
        send_col(1)

    wait_col(0)

    panel = jnp.concatenate([panel_cols(colpb, s) for s in range(3)], axis=1)
    for t in range(6):
        tile = jnp.concatenate([a_v[pl.ds(t * 384 + s, 128, stride=3), :] for s in range(3)], axis=1)
        zt = dot_nt(panel, tile)
        for g in range(8):
            zpart[g + 8 * (t % 2), t // 2] = zt[8 * g : 8 * g + 8, :]

    def reduce_to(p):
        k = lax.rem(z + spiral(lax.div(p, 2), 8), 8) * 2 + lax.rem(p, 2)
        dev = panel_owner(k)

        @pl.when(dev != c)
        def _():
            copy(zpart.at[k], zrecv.at[c], rs_s.at[k], rs_r.at[c], (r, dev)).start()

    loop(0, 16, reduce_to)

    part = jnp.where(owner, 0, 1)

    @pl.when(c != 0)
    def _():
        copy(chunk(mine, part), chunk(mine, part), sc_s.at[0], sc_r, (r, 0)).wait_recv()

    def pass_on(p):
        dev = col_peer(p)

        @pl.when(dev != 0)
        def _():
            copy(chunk(mine, part), chunk(mine, part), ag_s.at[p], ag_r.at[mine + 16 * part], (r, dev)).start()

    loop(0, 31, pass_on)

    def wait_rows(part):
        def one(k):
            @pl.when((c != 0) & ((k != mine) | (owner != (part == 0))))
            def _():
                copy(chunk(k, part), chunk(k, part), ag_s.at[0], ag_r.at[k + 16 * part], (r, 0)).wait_recv()

        loop(0, 16, one)

    wait_col(1)

    @pl.when(r == 0)
    def _():
        def arrived(p):
            dev = col_peer(p)
            copy(gpk, grecv.at[dev], g_s.at[p], g_r.at[dev], (r, dev)).wait_recv()

        loop(0, 31, arrived)
        gfin[...] = lax.fori_loop(1, 32, lambda i, total: total + grecv[i], grecv[0])
        loop(0, 15, lambda p: copy(gfin, gfin, gb_s.at[p], gb_r, (row_peer(p), c)).start())

    def send_corner(part):
        rows = pl.ds(NB * part, NB)

        @pl.when(r == 0)
        def _():
            p1[rows, :] = rowpb[0, 0, rows, :]

            def to(p):
                copy(p1.at[rows], p1.at[rows], p1_s.at[15 * part + p], p1_r.at[part], (row_peer(p), c)).start()

            loop(0, 15, to)

    def wait_corner(part):
        rows = pl.ds(NB * part, NB)

        @pl.when(r != 0)
        def _():
            copy(p1.at[rows], p1.at[rows], p1_s.at[0], p1_r.at[part], (0, c)).wait_recv()

    @pl.when(owner)
    def _():
        def arrived(p):
            dev = col_peer(p)
            copy(zpart.at[0], zrecv.at[dev], rs_s.at[0], rs_r.at[dev], (r, dev)).wait_recv()

        loop(0, 31, arrived)
        zrecv[c] = zpart[mine]
        zsum = lax.fori_loop(1, 32, lambda i, total: total + zrecv[i], zrecv[0])
        zrows[mine] = zsum
        there = r + 16 * my_h

        def to_cols(p):
            copy(zrows.at[mine], zcols.at[my_g], zc_s.at[p], zc_r.at[my_g], (row_peer(p), there)).start()

        loop(0, 15, to_cols)
        loop(
            0, 31, lambda p: copy(zrows.at[mine], zrows.at[mine], zr_s.at[p], zr_r.at[mine], (r, col_peer(p))).start()
        )
        wait_rows(0)
        send_corner(0)
        total = jnp.zeros((8, 128), F32)
        for i in range(3):
            rows = rowpb[my_h, i, 0:NB, :]
            total = total + dot_nt(zsum[i], jnp.concatenate([rows, jnp.zeros_like(rows)], axis=0))
        lane8 = lax.broadcasted_iota(jnp.int32, (8, 128), 1)
        total = total + jnp.where((r == 0) & (my_h == 0) & (lane8 >= NB), zsum[0], 0.0)
        hsend[0] = total
        hrecv[r] = total
        loop(
            0, 15, lambda p: copy(hsend.at[0], hrecv.at[r], h_s.at[p], h_r.at[r], (row_peer(p), c)).start()
        )

        def h_arrived(p):
            dev = row_peer(p)
            copy(hsend.at[0], hrecv.at[dev], h_s.at[0], h_r.at[dev], (dev, c)).wait_recv()

        loop(0, 15, h_arrived)
        hsum = lax.fori_loop(1, 16, lambda i, total: total + hrecv[i], hrecv[0])
        hall[mine] = hsum
        loop(0, 31, lambda p: copy(hall.at[mine], hall.at[mine], ha_s.at[p], ha_r.at[mine], (r, col_peer(p))).start())
        wait_rows(1)
        send_corner(1)

        @pl.when(r != 0)
        def _():
            copy(gfin, gfin, gb_s.at[0], gb_r, (0, c)).wait_recv()

        wait_corner(0)
        copy(c0, c0, c0_s.at[0], c0_r.at[0], (r, partner)).wait_recv()
        copy(om, om, c0_s.at[1], c0_r.at[1], (r, partner)).wait_recv()

    @pl.when(jnp.logical_not(owner))
    def _():
        wait_rows(0)
        send_corner(0)

        @pl.when(r != 0)
        def _():
            copy(gfin, gfin, gb_s.at[0], gb_r, (0, c)).wait_recv()

        packed = gfin[...]
        gram = jnp.concatenate([packed, pltpu.roll(packed, 64, 1)], axis=0)
        gram = jnp.where(lane < NB, gram, 0.0)
        ct[0:NB, :] = jnp.zeros((NB, 128), F32)
        factor_cholesky(gram, ct)
        c0[...] = jnp.transpose(ct[...])[0:NB, :]
        copy(c0, c0, c0_s.at[0], c0_r.at[0], (r, partner)).start()
        wait_corner(0)
        corner = p1[0:NB, :]
        om[...] = invert(gram + dot_nt(c0[...], jnp.concatenate([corner, jnp.zeros_like(corner)], axis=0)))
        copy(om, om, c0_s.at[1], c0_r.at[1], (r, partner)).start()
        wait_rows(1)
        send_corner(1)

    def z_arrived(k):
        @pl.when(jnp.logical_not(owner) | (k != mine))
        def _():
            copy(zrows.at[k], zrows.at[k], zr_s.at[0], zr_r.at[k], (r, c)).wait_recv()

    loop(0, 16, z_arrived)

    @pl.when(home)
    def _():
        zcols[...] = zrows[pl.ds(8 * lax.div(c, 16), 8)]

    @pl.when(jnp.logical_not(home))
    def _():
        loop(0, 8, lambda g: copy(zcols.at[g], zcols.at[g], zc_s.at[0], zc_r.at[g], (r, c)).wait_recv())

    @pl.when(r == 0)
    def _():
        def sent(part):
            rows = pl.ds(192 * part, 192)
            loop(
                0, 8,
                lambda q: copy(a_v.at[rows], colpb.at[rows], colp_s.at[8 * part + q], colp_r.at[part], (1, c)).wait_send(),
            )

        sent(0)
        sent(1)

    wait_corner(1)
    sub = lax.broadcasted_iota(jnp.int32, (NB, 128), 0)
    c0v = c0[...]
    unit = jnp.where(sub == lane, 1.0, 0.0)
    pad = jnp.zeros((NB, 128), F32)
    s_mat = dot_nn(om[...], jnp.concatenate([unit + c0v, pad], axis=0))
    c_cols = jnp.where(c == 0, c0v, 0.0)
    c_rows = jnp.where(r == 0, c0v, 0.0)

    def h_all(k):
        @pl.when(jnp.logical_not(owner) | (k != mine))
        def _():
            copy(hall.at[k], hall.at[k], ha_s.at[0], ha_r.at[k], (r, c)).wait_recv()

    loop(0, 16, h_all)
    top = (hall[0:8] + hall[8:16]).reshape(NB, 128)
    turned = jnp.transpose(jnp.concatenate([top, pad], axis=0))
    bottom = jnp.where(lane < NB, turned[NB:, :], p1[NB:, :])
    x_mat = dot_nt(dot_nn(s_mat, jnp.concatenate([top, bottom], axis=0)), jnp.concatenate([s_mat, pad], axis=0))
    right = []
    for s in range(3):
        n_t = panel_cols(colpb, s)
        if s == 0:
            n_t = n_t + c_cols
        zb = jnp.concatenate([zcols[:, s].reshape(NB, 128), colpb[pl.ds(192 + s, NB, stride=3), :]], axis=0)
        v_t = dot_nn(s_mat, zb) - dot_nn(x_mat, jnp.concatenate([n_t, pad], axis=0))
        right.append(jnp.concatenate([n_t, v_t], axis=0))
    right = jnp.concatenate(right, axis=1)
    for t in range(6):
        h, i = t % 2, t // 2
        n_t = rowpb[h, i, 0:NB, :]
        if t == 0:
            n_t = n_t + c_rows
        zb = jnp.concatenate([zrows[8 * h : 8 * h + 8, i].reshape(NB, 128), rowpb[h, i, NB:, :]], axis=0)
        left = jnp.transpose(jnp.concatenate([dot_nn(s_mat, zb), n_t], axis=0))
        change = dot_nn(left, right)
        for s in range(3):
            rows = pl.ds(t * 384 + s, 128, stride=3)
            a_v[rows, :] = a_v[rows, :] - change[:, 128 * s : 128 * s + 128]
        rows = pl.ds(t * 384, 384)
        pltpu.make_async_copy(a_v.at[rows], o_hbm.at[rows], out_sem.at[t]).start()

    @pl.when(r == 0)
    def _():
        loop(0, 31, lambda p: copy(gpk, grecv.at[c], g_s.at[p], g_r.at[c], (r, col_peer(p))).wait_send())
        loop(0, 15, lambda p: copy(gfin, gfin, gb_s.at[p], gb_r, (row_peer(p), c)).wait_send())
        rows = pl.ds(0, NB)
        loop(0, 30, lambda p: copy(p1.at[rows], p1.at[rows], p1_s.at[p], p1_r.at[0], (1, c)).wait_send())

    @pl.when((r != 0) & (core == 0))
    def _():
        rows = pl.ds(0, 192)
        loop(0, 2, lambda q: copy(colpb.at[rows], colpb.at[rows], fwd_s.at[q], colp_r.at[0], (r + 1, c)).wait_send())

    @pl.when(c == 0)
    def _():
        loop(1, 32, lambda k: copy(chunk(0, 0), chunk(0, 0), sc_s.at[k], sc_r, (r, 1)).wait_send())

    def reduced_sent(k):
        @pl.when(panel_owner(k) != c)
        def _():
            copy(zpart.at[k], zrecv.at[c], rs_s.at[k], rs_r.at[c], (r, panel_owner(k))).wait_send()

    loop(0, 16, reduced_sent)

    def passed_on(p):
        dev = col_peer(p)

        @pl.when(dev != 0)
        def _():
            copy(chunk(mine, part), chunk(mine, part), ag_s.at[p], ag_r.at[0], (r, dev)).wait_send()

    loop(0, 31, passed_on)

    @pl.when(owner)
    def _():
        loop(0, 15, lambda p: copy(zrows.at[mine], zcols.at[my_g], zc_s.at[p], zc_r.at[0], (row_peer(p), c)).wait_send())
        loop(0, 31, lambda p: copy(zrows.at[mine], zrows.at[0], zr_s.at[p], zr_r.at[0], (r, col_peer(p))).wait_send())
        loop(0, 15, lambda p: copy(hsend.at[0], hrecv.at[r], h_s.at[p], h_r.at[r], (row_peer(p), c)).wait_send())
        loop(0, 31, lambda p: copy(hall.at[mine], hall.at[0], ha_s.at[p], ha_r.at[0], (r, col_peer(p))).wait_send())

    @pl.when(jnp.logical_not(owner))
    def _():
        copy(c0, c0, c0_s.at[0], c0_r.at[0], (r, partner)).wait_send()
        copy(om, om, c0_s.at[1], c0_r.at[1], (r, partner)).wait_send()

    def stored(t):
        rows = pl.ds(0, 384)
        pltpu.make_async_copy(a_v.at[rows], o_hbm.at[rows], out_sem.at[t]).wait()

    loop(0, 6, stored)


def vmem(*shape):
    return pltpu.VMEM(shape, F32)


def dma(*shape):
    return pltpu.SemaphoreType.DMA(shape)


def body(hessian):
    flat = hessian.reshape(2304, 128)
    out = pl.pallas_call(
        kernel,
        out_shape=jax.ShapeDtypeStruct((2304, 128), F32),
        in_specs=[pl.BlockSpec(memory_space=pl.ANY)],
        out_specs=pl.BlockSpec(memory_space=pl.ANY),
        scratch_shapes=[
            vmem(2304, 128), vmem(384, 128), vmem(2, 3, 128, 128), vmem(16, 3, 8, 128), vmem(32, 3, 8, 128),
            vmem(16, 3, 8, 128), vmem(8, 3, 8, 128), vmem(32, 128), vmem(32, 32, 128), vmem(32, 128), vmem(128, 128),
            vmem(1, 8, 128), vmem(16, 8, 128), vmem(16, 8, 128), vmem(128, 128), vmem(64, 128), vmem(64, 128),
            dma(), dma(6), dma(16), dma(2), dma(2), dma(32), dma(), dma(31), dma(32), dma(16), dma(32), dma(31), dma(16),
            dma(15), dma(8), dma(31), dma(32), dma(15), dma(), dma(30), dma(2), dma(15), dma(16), dma(31), dma(16),
            dma(2), dma(2),
        ],
        compiler_params=pltpu.CompilerParams(collective_id=0, has_side_effects=True, vmem_limit_bytes=32 << 20),
        name="panel",
    )(flat)
    return out.reshape(hessian.shape)


def solution(mesh):
    return jax.shard_map(
        body,
        mesh=mesh,
        in_specs=(P(None, "row", None, None, "col", None),),
        out_specs=P(None, "row", None, None, "col", None),
        check_vma=False,
    )
```

time: 1190 us -> 74 us (0.06)
  the two profiles are of different devices: /device:TPU:1 before, /device:TPU:72 now
where the time goes in v1:
time: 74 us; the launch traced here: 73.9 us
  Pallas kernels  71.6 us (97%)
  local copies, waits for them, and re-layouts  2.29 us (3%)
    pallas_call x1, Pallas kernels, body(): pl.pallas_call(kernel, out_shape=jax.ShapeDtypeStruct((2304, 128), F32),...  71.6 us
    unnamed x3, local copies, waits for them, and re-layouts  2.29 us

profile of v1, /device:TPU:72, one launch (start us, length us, event | category | flops | bytes accessed | tf_op | source)
XLA Modules:
  0.0 73.9 jit_solution(16540553177904147318)
XLA Ops:
  0.0 0.0 copy-start
  0.0 1.3 %copy-done = f32[6,1,128,3,1,128]{5,4,3,2,1,0:T(1,128)S(1)} copy-done((f32[6,1,128,3,1,128]{5,4,3,2,1,0:T(1,128)S(1)}, f32[6,1,128,3,1,128]{5,4,3,2,1,0:T(1,128)}, u32[]{:S(2)}) %copy-start) | copy-done | bytes 1179672
  1.3 71.6 %panel.1 = f32[2304,128]{1,0:T(8,128)S(1)} custom-call(f32[2304,128]{1,0:T(8,128)S(1)} %bitcast.3), custom_call_target="tpu_custom_call" | custom-call | tf_op jit(solution)/shard_map/panel/pallas_call | solution.py:471
  72.8 1.0 %copy.5 = f32[6,1,128,3,1,128]{5,4,3,2,1,0:T(1,128)} copy(f32[6,1,128,3,1,128]{5,4,3,2,1,0:T(1,128)S(1)} %bitcast.2) | data formatting | bytes 2359296
Async XLA Ops:
  0.0 1.3 %copy-start = (f32[6,1,128,3,1,128]{5,4,3,2,1,0:T(1,128)S(1)}, f32[6,1,128,3,1,128]{5,4,3,2,1,0:T(1,128)}, u32[]{:S(2)}) copy-start(f32[6,1,128,3,1,128]{5,4,3,2,1,0:T(1,128)} %param.1) | copy-start | bytes 3538948

commit v2 on v1

v2 whole, which is shorter than its diff:
```python
import functools

import jax
import jax.numpy as jnp
from jax import lax
from jax.experimental import pallas as pl
from jax.experimental.pallas import tpu as pltpu
from jax.sharding import PartitionSpec as P

NB = 64
MESH = pl.DeviceIdType.MESH
HIGHEST = lax.Precision.HIGHEST
F32 = jnp.float32


def dot_nn(a, b):
    return lax.dot_general(a, b, (((1,), (0,)), ((), ())), precision=HIGHEST, preferred_element_type=F32)


def dot_nt(a, b):
    return lax.dot_general(a, b, (((1,), (1,)), ((), ())), precision=HIGHEST, preferred_element_type=F32)


def split(a):
    high = a.astype(jnp.bfloat16)
    return high, (a - high.astype(F32)).astype(jnp.bfloat16)


def dot3(a, b, dims):
    (ah, al), (bh, bl) = split(a), split(b)
    left = jnp.concatenate([ah, ah, al], axis=dims[0])
    right = jnp.concatenate([bh, bl, bh], axis=dims[1])
    return lax.dot_general(left, right, (((dims[0],), (dims[1],)), ((), ())), preferred_element_type=F32)


def spiral(q, n):
    return lax.rem(n // 2 + (1 - 2 * lax.rem(q, 2)) * lax.div(q + 1, 2), n)


def loop(lo, hi, f):
    def step(i, carry):
        f(i)
        return carry

    lax.fori_loop(lo, hi, step, 0)


def factor_cholesky(g, ct):
    lane1 = lax.broadcasted_iota(jnp.int32, (1, 128), 1)
    for k in range(NB):
        col = g[:, k : k + 1]
        row = g[k : k + 1, :]
        piv = g[k : k + 1, k : k + 1]
        ct[NB + k : NB + k + 1, :] = jnp.where((lane1 >= k) & (lane1 < NB), row * lax.rsqrt(piv), 0.0)
        if k < NB - 1:
            low = (k + 1) // 8 * 8
            part = g[low:, :] - col[low:, :] * (row / piv)
            g = part if low == 0 else jnp.concatenate([g[:low, :], part], axis=0)


def invert(m):
    lane1 = lax.broadcasted_iota(jnp.int32, (1, 128), 1)
    lane = lax.broadcasted_iota(jnp.int32, (NB, 128), 1)
    sub = lax.broadcasted_iota(jnp.int32, (NB, 128), 0)
    for k in range(NB):
        col = m[:, k : k + 1]
        row = m[k : k + 1, :]
        piv = m[k : k + 1, k : k + 1]
        scaled = jnp.where(lane1 == k, 1.0, row) / piv
        m = jnp.where(sub == k, scaled, jnp.where(lane == k, 0.0, m) - col * scaled)
    return m


def kernel(
    a_hbm, left_o, right_o, a_v, colpb, rowpb, zpart, zrecv, zrows, zcols, gx, gz, gfin, p1, hsend, hrecv, hall, ct, c0, om,
    load_s, colp_s, colp_r, fwd_s, sc_s, sc_r, ag_s, ag_r, rs_s, rs_r, zr_s, zr_r, zc_s, zc_r,
    g_s, g_r, p1_s, p1_r, h_s, h_r, ha_s, ha_r, c0_s, c0_r,
):
    r, c = lax.axis_index("row"), lax.axis_index("col")
    y, core = lax.div(r, 2), lax.rem(r, 2)
    z, x = lax.div(c, 4), lax.rem(c, 4)
    mine = lax.div(c, 2)
    owner = lax.rem(x + z, 2) == 0
    plain = jnp.logical_not(owner)
    my_g, my_h = lax.rem(mine, 8), lax.div(mine, 8)
    partner = c + 1 - 2 * lax.rem(c, 2)
    home = lax.rem(c, 16) == r
    lane = lax.broadcasted_iota(jnp.int32, (NB, 128), 1)

    def panel_owner(k):
        return 2 * k + lax.rem(lax.div(k, 2), 2)

    def other_owner(k):
        return 2 * k + 1 - lax.rem(lax.div(k, 2), 2)

    def col_peer(p):
        return lax.rem(z + spiral(lax.div(p, 4), 8), 8) * 4 + lax.rem(x + spiral(lax.rem(p, 4), 4), 4)

    def x_peer(p):
        return z * 4 + lax.rem(x + spiral(p, 4), 4)

    def z_peer(p):
        return lax.rem(z + spiral(p, 8), 8) * 4 + x

    def row_peer(p):
        return lax.rem(y + spiral(lax.div(p, 2), 8), 8) * 2 + lax.rem(core + 1 - lax.rem(p, 2), 2)

    def copy(src, dst, ssem, rsem, dev):
        return pltpu.make_async_remote_copy(
            src_ref=src, dst_ref=dst, send_sem=ssem, recv_sem=rsem, device_id=dev, device_id_type=MESH
        )

    def sent(ref, sem):
        copy(ref, ref, sem, sem, (r, partner)).wait_send()

    def arrived(ref, sem):
        copy(ref, ref, sem, sem, (r, partner)).wait_recv()

    def when(condition, f):
        pl.when(condition)(f)

    def chunk(k, part):
        rows = pl.multiple_of(lax.rem(k, 8) * 8 + part * NB, 8)
        return rowpb.at[lax.div(k, 8), :, pl.ds(rows, 8), :]

    def some(n):
        return zrecv.at[pl.ds(0, n)]

    load = pltpu.make_async_copy(a_hbm, a_v, load_s)
    load.start()
    barrier = pltpu.get_barrier_semaphore()

    def greet(dev):
        pl.semaphore_signal(barrier, inc=1, device_id=dev, device_id_type=MESH)

    loop(0, 31, lambda p: greet((r, col_peer(p))))
    loop(0, 15, lambda p: greet((row_peer(p), c)))

    @pl.when(jnp.logical_not(home))
    def _():
        loop(0, 8, lambda g: greet((lax.rem(c, 16), panel_owner(g + 8 * lax.div(c, 16)))))

    load.wait()

    def panel_cols(ref, s):
        return jnp.where((c == 0) & (s == 0) & (lane < NB), 0.0, ref[pl.ds(s, NB, stride=3), :])

    @pl.when(c == 0)
    def _():
        full = lax.broadcasted_iota(jnp.int32, (128, 128), 0)
        full_lane = lax.broadcasted_iota(jnp.int32, (128, 128), 1)
        for t in range(6):
            block = jnp.transpose(a_v[pl.ds(t * 384, 128, stride=3), :])
            if t == 0:
                block = jnp.where((r == 0) & (full < NB) & (full_lane < NB), 0.0, block)
            rowpb[t % 2, t // 2] = block

    @pl.when(r == 0)
    def _():
        panel = jnp.concatenate([panel_cols(a_v, s) for s in range(3)], axis=1)
        zero = jnp.zeros_like(panel)
        gx[x] = dot_nt(panel[:32], jnp.concatenate([panel, zero], axis=0)) + dot_nt(
            panel[32:], jnp.concatenate([zero, panel], axis=0)
        )

        @pl.when(c == 0)
        def _():
            p1[...] = a_v[pl.ds(3 * NB, NB, stride=3), :]

        colpb[...] = a_v[0:384, :]

    when(owner, lambda: pl.semaphore_wait(barrier, 61))
    when(plain, lambda: pl.semaphore_wait(barrier, 46))

    def send_col(part):
        rows = pl.ds(192 * part, 192)

        def to(q):
            other = 2 * spiral(q, 8) + jnp.where(q == 7, 1, 0)
            copy(a_v.at[rows], colpb.at[rows], colp_s.at[part], colp_r.at[part], (other, c)).start()

        loop(0, 8, to)

    def wait_col(part):
        rows = pl.ds(192 * part, 192)

        @pl.when(r != 0)
        def _():
            arrived(colpb.at[rows], colp_r.at[part])

            @pl.when(core == 0)
            def _():
                copy(colpb.at[rows], colpb.at[rows], fwd_s.at[part], colp_r.at[part], (r + 1, c)).start()

    def scatter(part):
        def to(k):
            dev = panel_owner(k) if part == 0 else other_owner(k)
            copy(chunk(k, part), chunk(k, part), sc_s, sc_r, (r, dev)).start()

        loop(1 - part, 16, to)

    when(r == 0, lambda: send_col(0))
    when(c == 0, lambda: scatter(0))

    @pl.when(r == 0)
    def _():
        loop(0, 3, lambda p: copy(gx.at[x], gx.at[x], g_s.at[0], g_r.at[0], (r, x_peer(p))).start())

        @pl.when(c == 0)
        def _():
            loop(0, 3, lambda p: copy(p1, p1, p1_s.at[0], p1_r, (r, x_peer(p))).start())

    when(c == 0, lambda: scatter(1))
    when(r == 0, lambda: send_col(1))

    wait_col(0)

    panel = jnp.concatenate([panel_cols(colpb, s) for s in range(3)], axis=1)
    for t in range(6):
        tile = jnp.concatenate([a_v[pl.ds(t * 384 + s, 128, stride=3), :] for s in range(3)], axis=1)
        zt = dot3(panel, tile, (1, 1))
        for g in range(8):
            zpart[g + 8 * (t % 2), t // 2] = zt[8 * g : 8 * g + 8, :]

    def reduce_to(p):
        k = lax.rem(z + spiral(lax.div(p, 2), 8), 8) * 2 + lax.rem(p, 2)
        dev = panel_owner(k)

        @pl.when(dev != c)
        def _():
            copy(zpart.at[k], zrecv.at[c], rs_s, rs_r, (r, dev)).start()

    loop(0, 16, reduce_to)

    @pl.when(r == 0)
    def _():
        arrived(gx.at[pl.ds(0, 3)], g_r.at[0])
        gz[z] = (gx[0] + gx[1]) + (gx[2] + gx[3])
        loop(0, 7, lambda p: copy(gz.at[z], gz.at[z], g_s.at[1], g_r.at[1], (r, z_peer(p))).start())

        @pl.when(z == 0)
        def _():
            when(x != 0, lambda: arrived(p1, p1_r))
            loop(0, 7, lambda p: copy(p1, p1, p1_s.at[1], p1_r, (r, z_peer(p))).start())

    def pass_on(part):
        when(c != 0, lambda: arrived(chunk(mine, part), sc_r))

        def to(p):
            dev = col_peer(p)

            @pl.when(dev != 0)
            def _():
                copy(chunk(mine, part), chunk(mine, part), ag_s, ag_r.at[part], (r, dev)).start()

        loop(0, 31, to)

    def wait_rows(part):
        holds = owner if part == 0 else plain
        when((c != 0) & holds, lambda: arrived(some(15), ag_r.at[part]))
        when((c != 0) & jnp.logical_not(holds), lambda: arrived(some(16), ag_r.at[part]))

    when(owner, lambda: pass_on(0))

    @pl.when(r == 0)
    def _():
        arrived(gz.at[pl.ds(0, 7)], g_r.at[1])
        gfin[...] = ((gz[0] + gz[1]) + (gz[2] + gz[3])) + ((gz[4] + gz[5]) + (gz[6] + gz[7]))
        loop(0, 15, lambda p: copy(gfin, gfin, g_s.at[2], g_r.at[2], (row_peer(p), c)).start())
        when(z != 0, lambda: arrived(p1, p1_r))
        loop(0, 15, lambda p: copy(p1, p1, p1_s.at[2], p1_r, (row_peer(p), c)).start())

    wait_col(1)

    @pl.when(owner)
    def _():
        arrived(some(31), rs_r)
        zrecv[c] = zpart[mine]
        zsum = lax.fori_loop(1, 32, lambda i, total: total + zrecv[i], zrecv[0])
        zrows[mine] = zsum
        wait_rows(0)
        rows = jnp.concatenate([rowpb[my_h, i, 0:NB, :] for i in range(3)], axis=1)
        total = dot_nt(
            jnp.concatenate([zsum[i] for i in range(3)], axis=1), jnp.concatenate([rows, jnp.zeros_like(rows)], axis=0)
        )
        lane8 = lax.broadcasted_iota(jnp.int32, (8, 128), 1)
        total = total + jnp.where((r == 0) & (my_h == 0) & (lane8 >= NB), zsum[0], 0.0)
        hsend[0] = total
        hrecv[r] = total
        loop(0, 15, lambda p: copy(hsend.at[0], hrecv.at[r], h_s, h_r, (row_peer(p), c)).start())
        there = r + 16 * my_h
        loop(0, 15, lambda p: copy(zrows.at[mine], zcols.at[my_g], zc_s, zc_r, (row_peer(p), there)).start())
        loop(0, 31, lambda p: copy(zrows.at[mine], zrows.at[mine], zr_s, zr_r, (r, col_peer(p))).start())
        arrived(hrecv.at[pl.ds(0, 15)], h_r)
        hall[mine] = lax.fori_loop(1, 16, lambda i, total: total + hrecv[i], hrecv[0])
        loop(0, 31, lambda p: copy(hall.at[mine], hall.at[mine], ha_s, ha_r, (r, col_peer(p))).start())
        wait_rows(1)

        @pl.when(r != 0)
        def _():
            arrived(gfin, g_r.at[2])
            arrived(p1, p1_r)

        arrived(c0, c0_r.at[0])
        arrived(om, c0_r.at[1])

    @pl.when(plain)
    def _():
        pass_on(1)
        when(r != 0, lambda: arrived(gfin, g_r.at[2]))
        packed = gfin[...]
        gram = jnp.concatenate([packed, pltpu.roll(packed, 64, 1)], axis=0)
        gram = jnp.where(lane < NB, gram, 0.0)
        ct[0:NB, :] = jnp.zeros((NB, 128), F32)
        factor_cholesky(gram, ct)
        c0[...] = jnp.transpose(ct[...])[0:NB, :]
        copy(c0, c0, c0_s.at[0], c0_r.at[0], (r, partner)).start()
        when(r != 0, lambda: arrived(p1, p1_r))
        corner = p1[...]
        product = dot_nn(pltpu.roll(c0[...], 64, 1), jnp.concatenate([corner, jnp.zeros_like(corner)], axis=0))
        om[...] = invert(gram + jnp.where(lane < NB, product, 0.0))
        copy(om, om, c0_s.at[1], c0_r.at[1], (r, partner)).start()
        wait_rows(0)
        wait_rows(1)

    sub = lax.broadcasted_iota(jnp.int32, (NB, 128), 0)
    c0v = c0[...]
    unit = jnp.where(sub == lane, 1.0, 0.0)
    pad = jnp.zeros((NB, 128), F32)
    s_mat = dot_nn(om[...], jnp.concatenate([unit + c0v, pad], axis=0))
    c_cols = jnp.where(c == 0, c0v, 0.0)
    c_rows = jnp.where(r == 0, c0v, 0.0)

    when(owner, lambda: arrived(some(15), zr_r))
    when(plain, lambda: arrived(some(16), zr_r))

    zb = []
    for t in range(6):
        h, i = t % 2, t // 2
        zb.append(
            jnp.concatenate([zrows[8 * h : 8 * h + 8, i].reshape(NB, 128), rowpb[h, i, NB:, :]], axis=0)
        )
        n_t = rowpb[h, i, 0:NB, :]
        if t == 0:
            n_t = n_t + c_rows
        left_o[t, NB:, :] = n_t
    w_rows = dot_nn(s_mat, jnp.concatenate(zb, axis=1))
    for t in range(6):
        left_o[t, 0:NB, :] = w_rows[:, 128 * t : 128 * t + 128]

    @pl.when(home)
    def _():
        zcols[...] = zrows[pl.ds(8 * lax.div(c, 16), 8)]

    when(jnp.logical_not(home), lambda: arrived(zcols, zc_r))

    zb = [
        jnp.concatenate([zcols[:, s].reshape(NB, 128), colpb[pl.ds(192 + s, NB, stride=3), :]], axis=0) for s in range(3)
    ]
    w_cols = dot_nn(s_mat, jnp.concatenate(zb, axis=1))
    n_cols = [panel_cols(colpb, s) for s in range(3)]
    n_cols = jnp.concatenate([n_cols[0] + c_cols] + n_cols[1:], axis=1)
    right_o[0:NB, :] = n_cols

    when(owner, lambda: arrived(hall.at[pl.ds(0, 15)], ha_r))
    when(plain, lambda: arrived(hall, ha_r))

    top = (hall[0:8] + hall[8:16]).reshape(NB, 128)
    turned = jnp.transpose(jnp.concatenate([top, pad], axis=0))
    bottom = jnp.where(lane < NB, turned[NB:, :], p1[...])
    x_mat = dot_nt(dot_nn(s_mat, jnp.concatenate([top, bottom], axis=0)), jnp.concatenate([s_mat, pad], axis=0))
    right_o[NB:, :] = w_cols - dot_nn(x_mat, jnp.concatenate([n_cols, jnp.zeros_like(n_cols)], axis=0))

    @pl.when(r == 0)
    def _():
        for part in range(2):
            sent(a_v.at[pl.ds(0, 1536)], colp_s.at[part])
        sent(gx.at[pl.ds(0, 3)], g_s.at[0])
        sent(gz.at[pl.ds(0, 7)], g_s.at[1])
        sent(a_v.at[pl.ds(0, 15 * 32)], g_s.at[2])
        when(c == 0, lambda: sent(a_v.at[pl.ds(0, 3 * NB)], p1_s.at[0]))
        when(z == 0, lambda: sent(a_v.at[pl.ds(0, 7 * NB)], p1_s.at[1]))
        sent(a_v.at[pl.ds(0, 15 * NB)], p1_s.at[2])

    @pl.when((r != 0) & (core == 0))
    def _():
        for part in range(2):
            sent(colpb.at[pl.ds(0, 192)], fwd_s.at[part])

    @pl.when(c == 0)
    def _():
        sent(some(31), sc_s)
        sent(some(31), ag_s)

    when(c != 0, lambda: sent(some(30), ag_s))

    @pl.when(owner)
    def _():
        sent(some(15), rs_s)
        sent(some(15), zc_s)
        sent(some(31), zr_s)
        sent(a_v.at[pl.ds(0, 15 * 8)], h_s)
        sent(a_v.at[pl.ds(0, 31 * 8)], ha_s)

    @pl.when(plain)
    def _():
        sent(some(16), rs_s)
        sent(c0, c0_s.at[0])
        sent(om, c0_s.at[1])


def update(a, left, right, out):
    high, low = split(right[...])
    columns = jnp.concatenate([high, low, high], axis=0)
    for t in range(6):
        high, low = split(jnp.transpose(left[t]))
        change = jnp.dot(jnp.concatenate([high, high, low], axis=1), columns, preferred_element_type=F32)
        for s in range(3):
            rows = pl.ds(t * 384 + s, 128, stride=3)
            out[rows, :] = a[rows, :] - change[:, 128 * s : 128 * s + 128]


def vmem(*shape):
    return pltpu.VMEM(shape, F32)


def dma(*shape):
    return pltpu.SemaphoreType.DMA(shape)


def body(hessian):
    flat = hessian.reshape(2304, 128)
    whole = pl.BlockSpec(memory_space=pltpu.VMEM)
    left, right = pl.pallas_call(
        kernel,
        out_shape=[jax.ShapeDtypeStruct((6, 128, 128), F32), jax.ShapeDtypeStruct((128, 384), F32)],
        in_specs=[pl.BlockSpec(memory_space=pltpu.HBM)],
        out_specs=[whole, whole],
        scratch_shapes=[
            vmem(2304, 128), vmem(384, 128), vmem(2, 3, 128, 128), vmem(16, 3, 8, 128), vmem(32, 3, 8, 128),
            vmem(16, 3, 8, 128), vmem(8, 3, 8, 128), vmem(4, 32, 128), vmem(8, 32, 128), vmem(32, 128),
            vmem(64, 128), vmem(1, 8, 128), vmem(16, 8, 128), vmem(16, 8, 128), vmem(128, 128), vmem(64, 128), vmem(64, 128),
            dma(), dma(2), dma(2), dma(2), dma(), dma(), dma(), dma(2), dma(), dma(), dma(), dma(), dma(), dma(),
            dma(3), dma(3), dma(3), dma(), dma(), dma(), dma(), dma(), dma(2), dma(2),
        ],
        compiler_params=pltpu.CompilerParams(collective_id=0, has_side_effects=True, vmem_limit_bytes=32 << 20),
        name="panel",
    )(flat)
    out = pl.pallas_call(
        update,
        out_shape=jax.ShapeDtypeStruct((2304, 128), F32),
        in_specs=[whole, whole, whole],
        out_specs=whole,
        compiler_params=pltpu.CompilerParams(vmem_limit_bytes=16 << 20),
        name="update",
    )(flat, left, right)
    return out.reshape(hessian.shape)


def solution(mesh):
    return jax.shard_map(
        body,
        mesh=mesh,
        in_specs=(P(None, "row", None, None, "col", None),),
        out_specs=P(None, "row", None, None, "col", None),
        check_vma=False,
    )
```

time: 74 us -> 59.6 us (0.81)
  the two profiles are of different devices: /device:TPU:72 before, /device:TPU:9 now
where the time goes in v2:
time: 59.6 us; the launch traced here: 59.5 us
  Pallas kernels  58.2 us (98%)
  local copies, waits for them, and re-layouts  1.27 us (2%)
    pallas_call x1, Pallas kernels, body(): pl.pallas_call(kernel, out_shape=[jax.ShapeDtypeStruct((6, 128, 128), F32...  56.6 us
    pallas_call x1, Pallas kernels, body(): pl.pallas_call(update, out_shape=jax.ShapeDtypeStruct((2304, 128), F32),...  1.63 us
    unnamed x2, local copies, waits for them, and re-layouts  1.27 us

profile of v2, /device:TPU:9, one launch (start us, length us, event | category | flops | bytes accessed | tf_op | source)
XLA Modules:
  0.0 59.5 jit_solution(10396203613694724046)
XLA Ops:
  0.0 0.0 copy-start
  0.0 1.3 %copy-done = f32[6,1,128,3,1,128]{5,4,3,2,1,0:T(1,128)S(1)} copy-done((f32[6,1,128,3,1,128]{5,4,3,2,1,0:T(1,128)S(1)}, f32[6,1,128,3,1,128]{5,4,3,2,1,0:T(1,128)}, u32[]{:S(2)}) %copy-start) | copy-done | bytes 1179672
  1.3 56.6 %panel.1 = (f32[6,128,128]{2,1,0:T(8,128)S(1)}, f32[128,384]{1,0:T(8,128)S(1)}) custom-call(f32[2304,128]{1,0:T(8,128)S(1)} %bitcast.2), custom_call_target="tpu_custom_call" | custom-call | tf_op jit(solution)/shard_map/panel/pallas_call | solution.py:434
  57.9 1.6 %update.1 = f32[2304,128]{1,0:T(8,128)} custom-call(f32[2304,128]{1,0:T(8,128)S(1)} %bitcast.3, f32[6,128,128]{2,1,0:T(8,128)S(1)} %get-tuple-element.7.left, f32[128,384]{1,0:T(8,128)S(1)} %get-tuple-element.8.right), custom_call_target="tpu_custom_call" | custom-call | tf_op jit(solution)/shard_map/update/pallas_call | solution.py:449
Async XLA Ops:
  0.0 1.3 %copy-start = (f32[6,1,128,3,1,128]{5,4,3,2,1,0:T(1,128)S(1)}, f32[6,1,128,3,1,128]{5,4,3,2,1,0:T(1,128)}, u32[]{:S(2)}) copy-start(f32[6,1,128,3,1,128]{5,4,3,2,1,0:T(1,128)} %param.1) | copy-start | bytes 3538948

commit v3 on v2

--- a/solution.py
+++ b/solution.py
@@ -19,6 +19,30 @@
 
 def dot_nt(a, b):
     return lax.dot_general(a, b, (((1,), (1,)), ((), ())), precision=HIGHEST, preferred_element_type=F32)
+
+
+def split(a):
+    high = a.astype(jnp.bfloat16)
+    return high, (a - high.astype(F32)).astype(jnp.bfloat16)
+
+
+def dot3(a, b, dims):
+    (ah, al), (bh, bl) = split(a), split(b)
+    left = jnp.concatenate([ah, ah, al], axis=dims[0])
+    right = jnp.concatenate([bh, bl, bh], axis=dims[1])
+    return lax.dot_general(left, right, (((dims[0],), (dims[1],)), ((), ())), preferred_element_type=F32)
+
+
+def split(a):
+    high = a.astype(jnp.bfloat16)
+    return high, (a - high.astype(F32)).astype(jnp.bfloat16)
+
+
+def dot3(a, b, dims):
+    (ah, al), (bh, bl) = split(a), split(b)
+    left = jnp.concatenate([ah, ah, al], axis=dims[0])
+    right = jnp.concatenate([bh, bl, bh], axis=dims[1])
+    return lax.dot_general(left, right, (((dims[0],), (dims[1],)), ((), ())), preferred_element_type=F32)
 
 
 def split(a):
@@ -133,8 +157,8 @@
     def greet(dev):
         pl.semaphore_signal(barrier, inc=1, device_id=dev, device_id_type=MESH)
 
+    loop(0, 15, lambda p: greet((row_peer(p), c)))
     loop(0, 31, lambda p: greet((r, col_peer(p))))
-    loop(0, 15, lambda p: greet((row_peer(p), c)))
 
     @pl.when(jnp.logical_not(home))
     def _():
@@ -243,24 +267,60 @@
             when(x != 0, lambda: arrived(p1, p1_r))
             loop(0, 7, lambda p: copy(p1, p1, p1_s.at[1], p1_r, (r, z_peer(p))).start())
 
-    def pass_on(part):
-        when(c != 0, lambda: arrived(chunk(mine, part), sc_r))
-
-        def to(p):
-            dev = col_peer(p)
-
-            @pl.when(dev != 0)
-            def _():
-                copy(chunk(mine, part), chunk(mine, part), ag_s, ag_r.at[part], (r, dev)).start()
-
-        loop(0, 31, to)
-
-    def wait_rows(part):
-        holds = owner if part == 0 else plain
-        when((c != 0) & holds, lambda: arrived(some(15), ag_r.at[part]))
-        when((c != 0) & jnp.logical_not(holds), lambda: arrived(some(16), ag_r.at[part]))
-
-    when(owner, lambda: pass_on(0))
+    def pass_to(k, part, dev, ssem, sem):
+        copy(chunk(k, part), chunk(k, part), ag_s.at[ssem], ag_r.at[sem], (r, dev)).start()
+
+    one = jnp.int32(1)
+    n_first, n_across, n_b = jnp.int32(0), jnp.int32(0), jnp.int32(0)
+
+    firsts = []
+    for p in range(7):
+        dev = panel_owner(8 * my_h + lax.rem(my_g + 4 + p + (1 if p > 3 else 0), 8))
+        firsts.append((dev, owner & (dev != 0)))
+    downs = []
+    for p in range(7):
+        dev = z_peer(p)
+        dev_z = lax.div(dev, 4)
+        first = (lax.rem(dev_z + x, 2) == 0) & (lax.div(dev_z, 4) == my_h)
+        downs.append((dev, owner & (dev != 0) & jnp.logical_not(first), plain & (dev != 0)))
+    acrosses = []
+    for p in range(3):
+        dev = x_peer(p)
+        dev_owner = lax.rem(lax.rem(dev, 4) + z, 2) == 0
+        for i in range(4):
+            k = 4 * i + 2 * lax.rem(x, 2) + lax.div(x, 2)
+            skip = dev_owner & (lax.div(z, 4) == i // 2)
+            k_b = 4 * i + 2 * lax.rem(x + 1, 2) + lax.div(x, 2)
+            acrosses.append((dev, k, (dev != 0) & jnp.logical_not(skip), k_b, dev != 0))
+
+    @pl.when(owner)
+    def _():
+        when(c != 0, lambda: arrived(chunk(mine, 0), sc_r))
+
+    for dev, go in firsts:
+        when(go, functools.partial(pass_to, mine, 0, dev, 0, 2))
+        n_first = n_first + jnp.where(go, one, 0)
+    for dev, go, go_b in downs:
+        when(go, functools.partial(pass_to, mine, 0, dev, 0, 0))
+        n_first = n_first + jnp.where(go, one, 0)
+
+    when(plain, lambda: arrived(chunk(mine, 1), sc_r))
+    for dev, go, go_b in downs:
+        when(go_b, functools.partial(pass_to, mine, 1, dev, 2, 1))
+        n_b = n_b + jnp.where(go_b, one, 0)
+    for dev, k, go, k_b, go_b in acrosses:
+        n_across = n_across + jnp.where(go, one, 0)
+        n_b = n_b + jnp.where(go_b, one, 0)
+
+    def pass_across():
+        for dev, k, go, k_b, go_b in acrosses:
+            when(go, functools.partial(pass_to, k, 0, dev, 1, 3))
+        for dev, k, go, k_b, go_b in acrosses:
+            when(go_b, functools.partial(pass_to, k_b, 1, dev, 2, 4))
+
+    def sent_some(n, sem, least, most):
+        for count in range(least, most + 1):
+            when(n == count, lambda count=count: sent(some(count), sem))
 
     @pl.when(r == 0)
     def _():
@@ -278,7 +338,7 @@
         zrecv[c] = zpart[mine]
         zsum = lax.fori_loop(1, 32, lambda i, total: total + zrecv[i], zrecv[0])
         zrows[mine] = zsum
-        wait_rows(0)
+        when(c != 0, lambda: arrived(some(7), ag_r.at[2]))
         rows = jnp.concatenate([rowpb[my_h, i, 0:NB, :] for i in range(3)], axis=1)
         total = dot_nt(
             jnp.concatenate([zsum[i] for i in range(3)], axis=1), jnp.concatenate([rows, jnp.zeros_like(rows)], axis=0)
@@ -291,10 +351,19 @@
         there = r + 16 * my_h
         loop(0, 15, lambda p: copy(zrows.at[mine], zcols.at[my_g], zc_s, zc_r, (row_peer(p), there)).start())
         loop(0, 31, lambda p: copy(zrows.at[mine], zrows.at[mine], zr_s, zr_r, (r, col_peer(p))).start())
+        @pl.when(c != 0)
+        def _():
+            arrived(some(2), ag_r.at[0])
+            arrived(some(4), ag_r.at[1])
+
+        pass_across()
         arrived(hrecv.at[pl.ds(0, 15)], h_r)
         hall[mine] = lax.fori_loop(1, 16, lambda i, total: total + hrecv[i], hrecv[0])
         loop(0, 31, lambda p: copy(hall.at[mine], hall.at[mine], ha_s, ha_r, (r, col_peer(p))).start())
-        wait_rows(1)
+        @pl.when(c != 0)
+        def _():
+            arrived(some(6), ag_r.at[3])
+            arrived(some(12), ag_r.at[4])
 
         @pl.when(r != 0)
         def _():
@@ -306,7 +375,6 @@
 
     @pl.when(plain)
     def _():
-        pass_on(1)
         when(r != 0, lambda: arrived(gfin, g_r.at[2]))
         packed = gfin[...]
         gram = jnp.concatenate([packed, pltpu.roll(packed, 64, 1)], axis=0)
@@ -315,13 +383,16 @@
         factor_cholesky(gram, ct)
         c0[...] = jnp.transpose(ct[...])[0:NB, :]
         copy(c0, c0, c0_s.at[0], c0_r.at[0], (r, partner)).start()
+        arrived(some(4), ag_r.at[0])
+        arrived(some(3), ag_r.at[1])
+        pass_across()
         when(r != 0, lambda: arrived(p1, p1_r))
         corner = p1[...]
         product = dot_nn(pltpu.roll(c0[...], 64, 1), jnp.concatenate([corner, jnp.zeros_like(corner)], axis=0))
         om[...] = invert(gram + jnp.where(lane < NB, product, 0.0))
         copy(om, om, c0_s.at[1], c0_r.at[1], (r, partner)).start()
-        wait_rows(0)
-        wait_rows(1)
+        arrived(some(12), ag_r.at[3])
+        arrived(some(12), ag_r.at[4])
 
     sub = lax.broadcasted_iota(jnp.int32, (NB, 128), 0)
     c0v = c0[...]
@@ -390,9 +461,10 @@
     @pl.when(c == 0)
     def _():
         sent(some(31), sc_s)
-        sent(some(31), ag_s)
-
-    when(c != 0, lambda: sent(some(30), ag_s))
+
+    when(owner, lambda: sent_some(n_first, ag_s.at[0], 10, 14))
+    sent_some(n_across, ag_s.at[1], 4, 12)
+    sent_some(n_b, ag_s.at[2], 8, 19)
 
     @pl.when(owner)
     def _():
@@ -440,10 +512,10 @@
             vmem(2304, 128), vmem(384, 128), vmem(2, 3, 128, 128), vmem(16, 3, 8, 128), vmem(32, 3, 8, 128),
             vmem(16, 3, 8, 128), vmem(8, 3, 8, 128), vmem(4, 32, 128), vmem(8, 32, 128), vmem(32, 128),
             vmem(64, 128), vmem(1, 8, 128), vmem(16, 8, 128), vmem(16, 8, 128), vmem(128, 128), vmem(64, 128), vmem(64, 128),
-            dma(), dma(2), dma(2), dma(2), dma(), dma(), dma(), dma(2), dma(), dma(), dma(), dma(), dma(), dma(),
+            dma(), dma(2), dma(2), dma(2), dma(), dma(), dma(3), dma(5), dma(), dma(), dma(), dma(), dma(), dma(),
             dma(3), dma(3), dma(3), dma(), dma(), dma(), dma(), dma(), dma(2), dma(2),
         ],
-        compiler_params=pltpu.CompilerParams(collective_id=0, has_side_effects=True, vmem_limit_bytes=32 << 20),
+        compiler_params=pltpu.CompilerParams(collective_id=0, has_side_effects=True, vmem_limit_bytes=54208 << 10),
         name="panel",
     )(flat)
     out = pl.pallas_call(

time: 59.6 us -> 51.7 us (0.87)
  Pallas kernels: 58.2 us -> 51.6 us
  local copies, waits for them, and re-layouts: 1.27 us -> 0.01 us
    pallas_call x1, Pallas kernels: 56.6 us -> 50 us  [body(): pl.pallas_call(kernel, out_shape=[jax.ShapeDtypeStruct((6, 128, 128), F32...]
    unnamed x2, local copies, waits for them, and re-layouts: 1.27 us -> 0.01 us
where the time goes in v3:
time: 51.7 us; the launch traced here: 51.6 us
  Pallas kernels  51.6 us (100%)
    pallas_call x1, Pallas kernels, body(): pl.pallas_call(kernel, out_shape=[jax.ShapeDtypeStruct((6, 128, 128), F32...  50 us
    pallas_call x1, Pallas kernels, body(): pl.pallas_call(update, out_shape=jax.ShapeDtypeStruct((2304, 128), F32),...  1.63 us

profile of v3, /device:TPU:9, one launch (start us, length us, event | category | flops | bytes accessed | tf_op | source)
XLA Modules:
  0.0 51.6 jit_solution(18073946074640125354)
XLA Ops:
  0.0 0.0 copy-start
  0.0 50.0 %panel.1 = (f32[6,128,128]{2,1,0:T(8,128)S(1)}, f32[128,384]{1,0:T(8,128)S(1)}) custom-call(f32[2304,128]{1,0:T(8,128)} %bitcast.2), custom_call_target="tpu_custom_call" | custom-call | tf_op jit(solution)/shard_map/panel/pallas_call | solution.py:506
  50.0 0.0 copy-done
  50.0 1.6 %update.1 = f32[2304,128]{1,0:T(8,128)} custom-call(f32[2304,128]{1,0:T(8,128)S(1)} %bitcast.3, f32[6,128,128]{2,1,0:T(8,128)S(1)} %get-tuple-element.7.left, f32[128,384]{1,0:T(8,128)S(1)} %get-tuple-element.8.right), custom_call_target="tpu_custom_call" | custom-call | tf_op jit(solution)/shard_map/update/pallas_call | solution.py:521
Async XLA Ops:
  0.0 50.0 %copy-start = (f32[6,1,128,3,1,128]{5,4,3,2,1,0:T(1,128)S(1)}, f32[6,1,128,3,1,128]{5,4,3,2,1,0:T(1,128)}, u32[]{:S(2)}) copy-start(f32[6,1,128,3,1,128]{5,4,3,2,1,0:T(1,128)} %param.1) | copy-start | bytes 3538948

commit v4 on v3

--- a/solution.py
+++ b/solution.py
@@ -69,9 +69,9 @@
     lax.fori_loop(lo, hi, step, 0)
 
 
-def factor_cholesky(g, ct):
+def factor_cholesky(g, ct, start, stop):
     lane1 = lax.broadcasted_iota(jnp.int32, (1, 128), 1)
-    for k in range(NB):
+    for k in range(start, stop):
         col = g[:, k : k + 1]
         row = g[k : k + 1, :]
         piv = g[k : k + 1, k : k + 1]
@@ -80,6 +80,7 @@
             low = (k + 1) // 8 * 8
             part = g[low:, :] - col[low:, :] * (row / piv)
             g = part if low == 0 else jnp.concatenate([g[:low, :], part], axis=0)
+    return g
 
 
 def invert(m):
@@ -158,11 +159,12 @@
         pl.semaphore_signal(barrier, inc=1, device_id=dev, device_id_type=MESH)
 
     loop(0, 15, lambda p: greet((row_peer(p), c)))
+
+    @pl.when(jnp.logical_not(home))
+    def _():
+        loop(0, 8, lambda g: greet((lax.rem(c, 16), panel_owner(g + 8 * lax.div(c, 16)))))
+
     loop(0, 31, lambda p: greet((r, col_peer(p))))
-
-    @pl.when(jnp.logical_not(home))
-    def _():
-        loop(0, 8, lambda g: greet((lax.rem(c, 16), panel_owner(g + 8 * lax.div(c, 16)))))
 
     load.wait()
 
@@ -196,8 +198,10 @@
     when(owner, lambda: pl.semaphore_wait(barrier, 61))
     when(plain, lambda: pl.semaphore_wait(barrier, 46))
 
+    parts = ((0, 96), (96, 96), (192, 192))
+
     def send_col(part):
-        rows = pl.ds(192 * part, 192)
+        rows = pl.ds(*parts[part])
 
         def to(q):
             other = 2 * spiral(q, 8) + jnp.where(q == 7, 1, 0)
@@ -206,7 +210,7 @@
         loop(0, 8, to)
 
     def wait_col(part):
-        rows = pl.ds(192 * part, 192)
+        rows = pl.ds(*parts[part])
 
         @pl.when(r != 0)
         def _():
@@ -223,11 +227,12 @@
 
         loop(1 - part, 16, to)
 
-    when(r == 0, lambda: send_col(0))
     when(c == 0, lambda: scatter(0))
 
     @pl.when(r == 0)
     def _():
+        send_col(0)
+        send_col(1)
         loop(0, 3, lambda p: copy(gx.at[x], gx.at[x], g_s.at[0], g_r.at[0], (r, x_peer(p))).start())
 
         @pl.when(c == 0)
@@ -235,9 +240,10 @@
             loop(0, 3, lambda p: copy(p1, p1, p1_s.at[0], p1_r, (r, x_peer(p))).start())
 
     when(c == 0, lambda: scatter(1))
-    when(r == 0, lambda: send_col(1))
+    when(r == 0, lambda: send_col(2))
 
     wait_col(0)
+    wait_col(1)
 
     panel = jnp.concatenate([panel_cols(colpb, s) for s in range(3)], axis=1)
     for t in range(6):
@@ -246,6 +252,17 @@
         for g in range(8):
             zpart[g + 8 * (t % 2), t // 2] = zt[8 * g : 8 * g + 8, :]
 
+    @pl.when(r == 0)
+    def _():
+        arrived(gx.at[pl.ds(0, 3)], g_r.at[0])
+        gz[z] = (gx[0] + gx[1]) + (gx[2] + gx[3])
+        loop(0, 7, lambda p: copy(gz.at[z], gz.at[z], g_s.at[1], g_r.at[1], (r, z_peer(p))).start())
+
+        @pl.when(z == 0)
+        def _():
+            when(x != 0, lambda: arrived(p1, p1_r))
+            loop(0, 7, lambda p: copy(p1, p1, p1_s.at[1], p1_r, (r, z_peer(p))).start())
+
     def reduce_to(p):
         k = lax.rem(z + spiral(lax.div(p, 2), 8), 8) * 2 + lax.rem(p, 2)
         dev = panel_owner(k)
@@ -255,17 +272,6 @@
             copy(zpart.at[k], zrecv.at[c], rs_s, rs_r, (r, dev)).start()
 
     loop(0, 16, reduce_to)
-
-    @pl.when(r == 0)
-    def _():
-        arrived(gx.at[pl.ds(0, 3)], g_r.at[0])
-        gz[z] = (gx[0] + gx[1]) + (gx[2] + gx[3])
-        loop(0, 7, lambda p: copy(gz.at[z], gz.at[z], g_s.at[1], g_r.at[1], (r, z_peer(p))).start())
-
-        @pl.when(z == 0)
-        def _():
-            when(x != 0, lambda: arrived(p1, p1_r))
-            loop(0, 7, lambda p: copy(p1, p1, p1_s.at[1], p1_r, (r, z_peer(p))).start())
 
     def pass_to(k, part, dev, ssem, sem):
         copy(chunk(k, part), chunk(k, part), ag_s.at[ssem], ag_r.at[sem], (r, dev)).start()
@@ -318,6 +324,13 @@
         for dev, k, go, k_b, go_b in acrosses:
             when(go_b, functools.partial(pass_to, k_b, 1, dev, 2, 4))
 
+    def z_across():
+        def to(p):
+            k = 4 * lax.rem(p, 4) + 2 * lax.rem(x, 2) + lax.div(x, 2)
+            copy(zrows.at[k], zrows.at[k], zr_s.at[1], zr_r.at[1], (r, x_peer(lax.div(p, 4)))).start()
+
+        loop(0, 12, to)
+
     def sent_some(n, sem, least, most):
         for count in range(least, most + 1):
             when(n == count, lambda count=count: sent(some(count), sem))
@@ -330,7 +343,7 @@
         when(z != 0, lambda: arrived(p1, p1_r))
         loop(0, 15, lambda p: copy(p1, p1, p1_s.at[2], p1_r, (row_peer(p), c)).start())
 
-    wait_col(1)
+    wait_col(2)
 
     @pl.when(owner)
     def _():
@@ -350,7 +363,7 @@
         loop(0, 15, lambda p: copy(hsend.at[0], hrecv.at[r], h_s, h_r, (row_peer(p), c)).start())
         there = r + 16 * my_h
         loop(0, 15, lambda p: copy(zrows.at[mine], zcols.at[my_g], zc_s, zc_r, (row_peer(p), there)).start())
-        loop(0, 31, lambda p: copy(zrows.at[mine], zrows.at[mine], zr_s, zr_r, (r, col_peer(p))).start())
+        loop(0, 7, lambda p: copy(zrows.at[mine], zrows.at[mine], zr_s.at[0], zr_r.at[0], (r, z_peer(p))).start())
         @pl.when(c != 0)
         def _():
             arrived(some(2), ag_r.at[0])
@@ -360,6 +373,8 @@
         arrived(hrecv.at[pl.ds(0, 15)], h_r)
         hall[mine] = lax.fori_loop(1, 16, lambda i, total: total + hrecv[i], hrecv[0])
         loop(0, 31, lambda p: copy(hall.at[mine], hall.at[mine], ha_s, ha_r, (r, col_peer(p))).start())
+        arrived(some(3), zr_r.at[0])
+        z_across()
         @pl.when(c != 0)
         def _():
             arrived(some(6), ag_r.at[3])
@@ -380,17 +395,20 @@
         gram = jnp.concatenate([packed, pltpu.roll(packed, 64, 1)], axis=0)
         gram = jnp.where(lane < NB, gram, 0.0)
         ct[0:NB, :] = jnp.zeros((NB, 128), F32)
-        factor_cholesky(gram, ct)
-        c0[...] = jnp.transpose(ct[...])[0:NB, :]
-        copy(c0, c0, c0_s.at[0], c0_r.at[0], (r, partner)).start()
+        rest = factor_cholesky(gram, ct, 0, 40)
         arrived(some(4), ag_r.at[0])
         arrived(some(3), ag_r.at[1])
         pass_across()
+        factor_cholesky(rest, ct, 40, NB)
+        c0[...] = jnp.transpose(ct[...])[0:NB, :]
+        copy(c0, c0, c0_s.at[0], c0_r.at[0], (r, partner)).start()
         when(r != 0, lambda: arrived(p1, p1_r))
         corner = p1[...]
         product = dot_nn(pltpu.roll(c0[...], 64, 1), jnp.concatenate([corner, jnp.zeros_like(corner)], axis=0))
         om[...] = invert(gram + jnp.where(lane < NB, product, 0.0))
         copy(om, om, c0_s.at[1], c0_r.at[1], (r, partner)).start()
+        arrived(some(4), zr_r.at[0])
+        z_across()
         arrived(some(12), ag_r.at[3])
         arrived(some(12), ag_r.at[4])
 
@@ -402,8 +420,7 @@
     c_cols = jnp.where(c == 0, c0v, 0.0)
     c_rows = jnp.where(r == 0, c0v, 0.0)
 
-    when(owner, lambda: arrived(some(15), zr_r))
-    when(plain, lambda: arrived(some(16), zr_r))
+    arrived(some(12), zr_r.at[1])
 
     zb = []
     for t in range(6):
@@ -415,7 +432,7 @@
         if t == 0:
             n_t = n_t + c_rows
         left_o[t, NB:, :] = n_t
-    w_rows = dot_nn(s_mat, jnp.concatenate(zb, axis=1))
+    w_rows = dot3(s_mat, jnp.concatenate(zb, axis=1), (1, 0))
     for t in range(6):
         left_o[t, 0:NB, :] = w_rows[:, 128 * t : 128 * t + 128]
 
@@ -428,10 +445,12 @@
     zb = [
         jnp.concatenate([zcols[:, s].reshape(NB, 128), colpb[pl.ds(192 + s, NB, stride=3), :]], axis=0) for s in range(3)
     ]
-    w_cols = dot_nn(s_mat, jnp.concatenate(zb, axis=1))
+    w_cols = dot3(s_mat, jnp.concatenate(zb, axis=1), (1, 0))
     n_cols = [panel_cols(colpb, s) for s in range(3)]
     n_cols = jnp.concatenate([n_cols[0] + c_cols] + n_cols[1:], axis=1)
     right_o[0:NB, :] = n_cols
+    s_turned = jnp.transpose(jnp.concatenate([s_mat, pad], axis=0))
+    sn_cols = dot3(s_turned[:, 0:NB], n_cols, (1, 0))
 
     when(owner, lambda: arrived(hall.at[pl.ds(0, 15)], ha_r))
     when(plain, lambda: arrived(hall, ha_r))
@@ -439,13 +458,13 @@
     top = (hall[0:8] + hall[8:16]).reshape(NB, 128)
     turned = jnp.transpose(jnp.concatenate([top, pad], axis=0))
     bottom = jnp.where(lane < NB, turned[NB:, :], p1[...])
-    x_mat = dot_nt(dot_nn(s_mat, jnp.concatenate([top, bottom], axis=0)), jnp.concatenate([s_mat, pad], axis=0))
-    right_o[NB:, :] = w_cols - dot_nn(x_mat, jnp.concatenate([n_cols, jnp.zeros_like(n_cols)], axis=0))
+    inner = dot3(jnp.concatenate([top, bottom], axis=0), sn_cols, (1, 0))
+    right_o[NB:, :] = w_cols - dot3(s_mat, inner, (1, 0))
 
     @pl.when(r == 0)
     def _():
-        for part in range(2):
-            sent(a_v.at[pl.ds(0, 1536)], colp_s.at[part])
+        for part in range(3):
+            sent(a_v.at[pl.ds(0, 8 * parts[part][1])], colp_s.at[part])
         sent(gx.at[pl.ds(0, 3)], g_s.at[0])
         sent(gz.at[pl.ds(0, 7)], g_s.at[1])
         sent(a_v.at[pl.ds(0, 15 * 32)], g_s.at[2])
@@ -455,8 +474,8 @@
 
     @pl.when((r != 0) & (core == 0))
     def _():
-        for part in range(2):
-            sent(colpb.at[pl.ds(0, 192)], fwd_s.at[part])
+        for part in range(3):
+            sent(colpb.at[pl.ds(*parts[part])], fwd_s.at[part])
 
     @pl.when(c == 0)
     def _():
@@ -464,13 +483,14 @@
 
     when(owner, lambda: sent_some(n_first, ag_s.at[0], 10, 14))
     sent_some(n_across, ag_s.at[1], 4, 12)
+    sent(some(12), zr_s.at[1])
     sent_some(n_b, ag_s.at[2], 8, 19)
 
     @pl.when(owner)
     def _():
         sent(some(15), rs_s)
         sent(some(15), zc_s)
-        sent(some(31), zr_s)
+        sent(some(7), zr_s.at[0])
         sent(a_v.at[pl.ds(0, 15 * 8)], h_s)
         sent(a_v.at[pl.ds(0, 31 * 8)], ha_s)
 
@@ -481,7 +501,7 @@
         sent(om, c0_s.at[1])
 
 
-def update(a, left, right, out):
+def update(a, left, right, out, tiles, sems):
     high, low = split(right[...])
     columns = jnp.concatenate([high, low, high], axis=0)
     for t in range(6):
@@ -489,7 +509,12 @@
         change = jnp.dot(jnp.concatenate([high, high, low], axis=1), columns, preferred_element_type=F32)
         for s in range(3):
             rows = pl.ds(t * 384 + s, 128, stride=3)
-            out[rows, :] = a[rows, :] - change[:, 128 * s : 128 * s + 128]
+            tiles[rows, :] = a[rows, :] - change[:, 128 * s : 128 * s + 128]
+        rows = pl.ds(t * 384, 384)
+        pltpu.make_async_copy(tiles.at[rows], out.at[rows], sems.at[t]).start()
+    for t in range(6):
+        rows = pl.ds(t * 384, 384)
+        pltpu.make_async_copy(tiles.at[rows], out.at[rows], sems.at[t]).wait()
 
 
 def vmem(*shape):
@@ -512,7 +537,7 @@
             vmem(2304, 128), vmem(384, 128), vmem(2, 3, 128, 128), vmem(16, 3, 8, 128), vmem(32, 3, 8, 128),
             vmem(16, 3, 8, 128), vmem(8, 3, 8, 128), vmem(4, 32, 128), vmem(8, 32, 128), vmem(32, 128),
             vmem(64, 128), vmem(1, 8, 128), vmem(16, 8, 128), vmem(16, 8, 128), vmem(128, 128), vmem(64, 128), vmem(64, 128),
-            dma(), dma(2), dma(2), dma(2), dma(), dma(), dma(3), dma(5), dma(), dma(), dma(), dma(), dma(), dma(),
+            dma(), dma(3), dma(3), dma(3), dma(), dma(), dma(3), dma(5), dma(), dma(), dma(2), dma(2), dma(), dma(),
             dma(3), dma(3), dma(3), dma(), dma(), dma(), dma(), dma(), dma(2), dma(2),
         ],
         compiler_params=pltpu.CompilerParams(collective_id=0, has_side_effects=True, vmem_limit_bytes=54208 << 10),
@@ -522,7 +547,8 @@
         update,
         out_shape=jax.ShapeDtypeStruct((2304, 128), F32),
         in_specs=[whole, whole, whole],
-        out_specs=whole,
+        out_specs=pl.BlockSpec(memory_space=pltpu.HBM),
+        scratch_shapes=[vmem(2304, 128), dma(6)],
         compiler_params=pltpu.CompilerParams(vmem_limit_bytes=16 << 20),
         name="update",
     )(flat, left, right)

time: 51.7 us -> 48.4 us (0.936)
  the two profiles are of different devices: /device:TPU:9 before, /device:TPU:1 now
where the time goes in v4:
time: 48.4 us; the launch traced here: 48.3 us
  Pallas kernels  48.3 us (100%)
    pallas_call x1, Pallas kernels, body(): pl.pallas_call(kernel, out_shape=[jax.ShapeDtypeStruct((6, 128, 128), F32...  47 us
    pallas_call x1, Pallas kernels, body(): pl.pallas_call(update, out_shape=jax.ShapeDtypeStruct((2304, 128), F32),...  1.34 us

profile of v4, /device:TPU:1, one launch (start us, length us, event | category | flops | bytes accessed | tf_op | source)
XLA Modules:
  0.0 48.3 jit_solution(4050809135023068519)
XLA Ops:
  0.0 0.0 copy-start
  0.0 47.0 %panel.1 = (f32[6,128,128]{2,1,0:T(8,128)S(1)}, f32[128,384]{1,0:T(8,128)S(1)}) custom-call(f32[2304,128]{1,0:T(8,128)} %bitcast.2), custom_call_target="tpu_custom_call" | custom-call | tf_op jit(solution)/shard_map/panel/pallas_call | solution.py:531
  47.0 0.0 copy-done
  47.0 1.3 %update.1 = f32[2304,128]{1,0:T(8,128)} custom-call(f32[2304,128]{1,0:T(8,128)S(1)} %bitcast.3, f32[6,128,128]{2,1,0:T(8,128)S(1)} %get-tuple-element.7.left, f32[128,384]{1,0:T(8,128)S(1)} %get-tuple-element.8.right), custom_call_target="tpu_custom_call" | custom-call | tf_op jit(solution)/shard_map/update/pallas_call | solution.py:546
Async XLA Ops:
  0.0 47.0 %copy-start = (f32[6,1,128,3,1,128]{5,4,3,2,1,0:T(1,128)S(1)}, f32[6,1,128,3,1,128]{5,4,3,2,1,0:T(1,128)}, u32[]{:S(2)}) copy-start(f32[6,1,128,3,1,128]{5,4,3,2,1,0:T(1,128)} %param.1) | copy-start | bytes 3538948

commit v5 on v4

--- a/solution.py
+++ b/solution.py
@@ -69,30 +69,42 @@
     lax.fori_loop(lo, hi, step, 0)
 
 
-def factor_cholesky(g, ct, start, stop):
+def factor_cholesky(g, ct):
     lane1 = lax.broadcasted_iota(jnp.int32, (1, 128), 1)
-    for k in range(start, stop):
-        col = g[:, k : k + 1]
-        row = g[k : k + 1, :]
-        piv = g[k : k + 1, k : k + 1]
-        ct[NB + k : NB + k + 1, :] = jnp.where((lane1 >= k) & (lane1 < NB), row * lax.rsqrt(piv), 0.0)
-        if k < NB - 1:
-            low = (k + 1) // 8 * 8
-            part = g[low:, :] - col[low:, :] * (row / piv)
-            g = part if low == 0 else jnp.concatenate([g[:low, :], part], axis=0)
-    return g
+    for first in range(0, NB, 8):
+        rest = g[first:, :]
+        cols = [jnp.broadcast_to(rest[:, first + j : first + j + 1], rest.shape) for j in range(8)]
+        rows = [rest[j : j + 1, :] for j in range(8)]
+        for j in range(8):
+            k = first + j
+            pivot = cols[j][j : j + 1, :]
+            inverse = 1.0 / pivot
+            scaled = rows[j] * inverse
+            ct[NB + k : NB + k + 1, :] = jnp.where((lane1 >= k) & (lane1 < NB), rows[j] * lax.rsqrt(pivot), 0.0)
+            for i in range(j + 1, 8):
+                factor = cols[i][j : j + 1, :] * inverse
+                rows[i] = rows[i] - cols[j][i : i + 1, :] * scaled
+                cols[i] = cols[i] - cols[j] * factor
+            rest = rest - cols[j] * scaled
+        g = rest if first == 0 else jnp.concatenate([g[:first, :], rest], axis=0)
 
 
 def invert(m):
     lane1 = lax.broadcasted_iota(jnp.int32, (1, 128), 1)
     lane = lax.broadcasted_iota(jnp.int32, (NB, 128), 1)
     sub = lax.broadcasted_iota(jnp.int32, (NB, 128), 0)
-    for k in range(NB):
-        col = m[:, k : k + 1]
-        row = m[k : k + 1, :]
-        piv = m[k : k + 1, k : k + 1]
-        scaled = jnp.where(lane1 == k, 1.0, row) / piv
-        m = jnp.where(sub == k, scaled, jnp.where(lane == k, 0.0, m) - col * scaled)
+    for first in range(0, NB, 8):
+        cols = [jnp.broadcast_to(m[:, first + j : first + j + 1], (NB, 128)) for j in range(8)]
+        rows = [m[first + j : first + j + 1, :] for j in range(8)]
+        for j in range(8):
+            k = first + j
+            inverse = 1.0 / cols[j][k : k + 1, :]
+            scaled = jnp.where(lane1 == k, 1.0, rows[j]) * inverse
+            for i in range(j + 1, 8):
+                factor = cols[i][k : k + 1, :] * inverse
+                rows[i] = jnp.where(lane1 == k, 0.0, rows[i]) - cols[j][first + i : first + i + 1, :] * scaled
+                cols[i] = jnp.where(sub == k, factor, cols[i] - cols[j] * factor)
+            m = jnp.where(sub == k, scaled, jnp.where(lane == k, 0.0, m) - cols[j] * scaled)
     return m
 
 
@@ -121,6 +133,10 @@
     def col_peer(p):
         return lax.rem(z + spiral(lax.div(p, 4), 8), 8) * 4 + lax.rem(x + spiral(lax.rem(p, 4), 4), 4)
 
+    def early_peer(p):
+        place = z * 4 + x
+        return p + jnp.where(p >= place, 1, 0)
+
     def x_peer(p):
         return z * 4 + lax.rem(x + spiral(p, 4), 4)
 
@@ -198,7 +214,7 @@
     when(owner, lambda: pl.semaphore_wait(barrier, 61))
     when(plain, lambda: pl.semaphore_wait(barrier, 46))
 
-    parts = ((0, 96), (96, 96), (192, 192))
+    parts = ((0, 192), (192, 192))
 
     def send_col(part):
         rows = pl.ds(*parts[part])
@@ -221,18 +237,18 @@
                 copy(colpb.at[rows], colpb.at[rows], fwd_s.at[part], colp_r.at[part], (r + 1, c)).start()
 
     def scatter(part):
-        def to(k):
+        def to(p):
+            k = 2 * spiral(lax.div(p, 2), 8) + 1 - lax.rem(p, 2)
             dev = panel_owner(k) if part == 0 else other_owner(k)
             copy(chunk(k, part), chunk(k, part), sc_s, sc_r, (r, dev)).start()
 
-        loop(1 - part, 16, to)
+        loop(0, 15 + part, to)
 
     when(c == 0, lambda: scatter(0))
 
     @pl.when(r == 0)
     def _():
         send_col(0)
-        send_col(1)
         loop(0, 3, lambda p: copy(gx.at[x], gx.at[x], g_s.at[0], g_r.at[0], (r, x_peer(p))).start())
 
         @pl.when(c == 0)
@@ -240,38 +256,8 @@
             loop(0, 3, lambda p: copy(p1, p1, p1_s.at[0], p1_r, (r, x_peer(p))).start())
 
     when(c == 0, lambda: scatter(1))
-    when(r == 0, lambda: send_col(2))
 
     wait_col(0)
-    wait_col(1)
-
-    panel = jnp.concatenate([panel_cols(colpb, s) for s in range(3)], axis=1)
-    for t in range(6):
-        tile = jnp.concatenate([a_v[pl.ds(t * 384 + s, 128, stride=3), :] for s in range(3)], axis=1)
-        zt = dot3(panel, tile, (1, 1))
-        for g in range(8):
-            zpart[g + 8 * (t % 2), t // 2] = zt[8 * g : 8 * g + 8, :]
-
-    @pl.when(r == 0)
-    def _():
-        arrived(gx.at[pl.ds(0, 3)], g_r.at[0])
-        gz[z] = (gx[0] + gx[1]) + (gx[2] + gx[3])
-        loop(0, 7, lambda p: copy(gz.at[z], gz.at[z], g_s.at[1], g_r.at[1], (r, z_peer(p))).start())
-
-        @pl.when(z == 0)
-        def _():
-            when(x != 0, lambda: arrived(p1, p1_r))
-            loop(0, 7, lambda p: copy(p1, p1, p1_s.at[1], p1_r, (r, z_peer(p))).start())
-
-    def reduce_to(p):
-        k = lax.rem(z + spiral(lax.div(p, 2), 8), 8) * 2 + lax.rem(p, 2)
-        dev = panel_owner(k)
-
-        @pl.when(dev != c)
-        def _():
-            copy(zpart.at[k], zrecv.at[c], rs_s, rs_r, (r, dev)).start()
-
-    loop(0, 16, reduce_to)
 
     def pass_to(k, part, dev, ssem, sem):
         copy(chunk(k, part), chunk(k, part), ag_s.at[ssem], ag_r.at[sem], (r, dev)).start()
@@ -299,6 +285,33 @@
             k_b = 4 * i + 2 * lax.rem(x + 1, 2) + lax.div(x, 2)
             acrosses.append((dev, k, (dev != 0) & jnp.logical_not(skip), k_b, dev != 0))
 
+    panel = jnp.concatenate([panel_cols(colpb, s) for s in range(3)], axis=1)
+    def share(t):
+        tile = jnp.concatenate([a_v[pl.ds(t * 384 + s, 128, stride=3), :] for s in range(3)], axis=1)
+        zt = dot3(panel, tile, (1, 1))
+        for g in range(8):
+            zpart[g + 8 * (t % 2), t // 2] = zt[8 * g : 8 * g + 8, :]
+
+    def reduce_to(k):
+        dev = panel_owner(k)
+
+        @pl.when(dev != c)
+        def _():
+            copy(zpart.at[k], zrecv.at[c], rs_s, rs_r, (r, dev)).start()
+
+    for t in (0, 2, 4):
+        share(t)
+    @pl.when(r == 0)
+    def _():
+        arrived(gx.at[pl.ds(0, 3)], g_r.at[0])
+        gz[z] = (gx[0] + gx[1]) + (gx[2] + gx[3])
+        loop(0, 7, lambda p: copy(gz.at[z], gz.at[z], g_s.at[1], g_r.at[1], (r, z_peer(p))).start())
+
+        @pl.when(z == 0)
+        def _():
+            when(x != 0, lambda: arrived(p1, p1_r))
+            loop(0, 7, lambda p: copy(p1, p1, p1_s.at[1], p1_r, (r, z_peer(p))).start())
+
     @pl.when(owner)
     def _():
         when(c != 0, lambda: arrived(chunk(mine, 0), sc_r))
@@ -306,14 +319,17 @@
     for dev, go in firsts:
         when(go, functools.partial(pass_to, mine, 0, dev, 0, 2))
         n_first = n_first + jnp.where(go, one, 0)
+    loop(0, 8, reduce_to)
+    for t in (1, 3, 5):
+        share(t)
+    loop(8, 16, reduce_to)
+
+    when(r == 0, lambda: send_col(1))
+
     for dev, go, go_b in downs:
         when(go, functools.partial(pass_to, mine, 0, dev, 0, 0))
         n_first = n_first + jnp.where(go, one, 0)
 
-    when(plain, lambda: arrived(chunk(mine, 1), sc_r))
-    for dev, go, go_b in downs:
-        when(go_b, functools.partial(pass_to, mine, 1, dev, 2, 1))
-        n_b = n_b + jnp.where(go_b, one, 0)
     for dev, k, go, k_b, go_b in acrosses:
         n_across = n_across + jnp.where(go, one, 0)
         n_b = n_b + jnp.where(go_b, one, 0)
@@ -335,6 +351,9 @@
         for count in range(least, most + 1):
             when(n == count, lambda count=count: sent(some(count), sem))
 
+    for dev, go, go_b in downs:
+        n_b = n_b + jnp.where(go_b, one, 0)
+
     @pl.when(r == 0)
     def _():
         arrived(gz.at[pl.ds(0, 7)], g_r.at[1])
@@ -343,7 +362,6 @@
         when(z != 0, lambda: arrived(p1, p1_r))
         loop(0, 15, lambda p: copy(p1, p1, p1_s.at[2], p1_r, (row_peer(p), c)).start())
 
-    wait_col(2)
 
     @pl.when(owner)
     def _():
@@ -353,8 +371,10 @@
         zrows[mine] = zsum
         when(c != 0, lambda: arrived(some(7), ag_r.at[2]))
         rows = jnp.concatenate([rowpb[my_h, i, 0:NB, :] for i in range(3)], axis=1)
-        total = dot_nt(
-            jnp.concatenate([zsum[i] for i in range(3)], axis=1), jnp.concatenate([rows, jnp.zeros_like(rows)], axis=0)
+        total = dot3(
+            jnp.concatenate([zsum[i] for i in range(3)], axis=1),
+            jnp.concatenate([rows, jnp.zeros_like(rows)], axis=0),
+            (1, 1),
         )
         lane8 = lax.broadcasted_iota(jnp.int32, (8, 128), 1)
         total = total + jnp.where((r == 0) & (my_h == 0) & (lane8 >= NB), zsum[0], 0.0)
@@ -364,6 +384,7 @@
         there = r + 16 * my_h
         loop(0, 15, lambda p: copy(zrows.at[mine], zcols.at[my_g], zc_s, zc_r, (row_peer(p), there)).start())
         loop(0, 7, lambda p: copy(zrows.at[mine], zrows.at[mine], zr_s.at[0], zr_r.at[0], (r, z_peer(p))).start())
+        wait_col(1)
         @pl.when(c != 0)
         def _():
             arrived(some(2), ag_r.at[0])
@@ -372,7 +393,7 @@
         pass_across()
         arrived(hrecv.at[pl.ds(0, 15)], h_r)
         hall[mine] = lax.fori_loop(1, 16, lambda i, total: total + hrecv[i], hrecv[0])
-        loop(0, 31, lambda p: copy(hall.at[mine], hall.at[mine], ha_s, ha_r, (r, col_peer(p))).start())
+        loop(0, 31, lambda p: copy(hall.at[mine], hall.at[mine], ha_s, ha_r, (r, early_peer(p))).start())
         arrived(some(3), zr_r.at[0])
         z_across()
         @pl.when(c != 0)
@@ -391,22 +412,26 @@
     @pl.when(plain)
     def _():
         when(r != 0, lambda: arrived(gfin, g_r.at[2]))
+        arrived(chunk(mine, 1), sc_r)
+        for dev, go, go_b in downs:
+            when(go_b, functools.partial(pass_to, mine, 1, dev, 2, 1))
         packed = gfin[...]
         gram = jnp.concatenate([packed, pltpu.roll(packed, 64, 1)], axis=0)
         gram = jnp.where(lane < NB, gram, 0.0)
         ct[0:NB, :] = jnp.zeros((NB, 128), F32)
-        rest = factor_cholesky(gram, ct, 0, 40)
-        arrived(some(4), ag_r.at[0])
-        arrived(some(3), ag_r.at[1])
-        pass_across()
-        factor_cholesky(rest, ct, 40, NB)
+        factor_cholesky(gram, ct)
         c0[...] = jnp.transpose(ct[...])[0:NB, :]
         copy(c0, c0, c0_s.at[0], c0_r.at[0], (r, partner)).start()
         when(r != 0, lambda: arrived(p1, p1_r))
         corner = p1[...]
         product = dot_nn(pltpu.roll(c0[...], 64, 1), jnp.concatenate([corner, jnp.zeros_like(corner)], axis=0))
-        om[...] = invert(gram + jnp.where(lane < NB, product, 0.0))
+        whole = invert(gram + jnp.where(lane < NB, product, 0.0))
+        om[...] = whole[0:32, :] + pltpu.roll(whole[32:, :], 64, 1)
         copy(om, om, c0_s.at[1], c0_r.at[1], (r, partner)).start()
+        wait_col(1)
+        arrived(some(4), ag_r.at[0])
+        arrived(some(3), ag_r.at[1])
+        pass_across()
         arrived(some(4), zr_r.at[0])
         z_across()
         arrived(some(12), ag_r.at[3])
@@ -416,13 +441,15 @@
     c0v = c0[...]
     unit = jnp.where(sub == lane, 1.0, 0.0)
     pad = jnp.zeros((NB, 128), F32)
-    s_mat = dot_nn(om[...], jnp.concatenate([unit + c0v, pad], axis=0))
+    packed_om = om[...]
+    inverse = jnp.where(lane < NB, jnp.concatenate([packed_om, pltpu.roll(packed_om, 64, 1)], axis=0), 0.0)
+    s_mat = dot_nn(inverse, jnp.concatenate([unit + c0v, pad], axis=0))
     c_cols = jnp.where(c == 0, c0v, 0.0)
     c_rows = jnp.where(r == 0, c0v, 0.0)
 
     arrived(some(12), zr_r.at[1])
 
-    zb = []
+    zb, n_rows = [], []
     for t in range(6):
         h, i = t % 2, t // 2
         zb.append(
@@ -431,10 +458,12 @@
         n_t = rowpb[h, i, 0:NB, :]
         if t == 0:
             n_t = n_t + c_rows
-        left_o[t, NB:, :] = n_t
+        n_rows.append(n_t)
     w_rows = dot3(s_mat, jnp.concatenate(zb, axis=1), (1, 0))
     for t in range(6):
-        left_o[t, 0:NB, :] = w_rows[:, 128 * t : 128 * t + 128]
+        rows = jnp.concatenate([w_rows[:, 128 * t : 128 * t + 128], n_rows[t]], axis=0)
+        high, low = split(jnp.transpose(rows))
+        left_o[t] = jnp.concatenate([high, high, low], axis=1)
 
     @pl.when(home)
     def _():
@@ -463,7 +492,7 @@
 
     @pl.when(r == 0)
     def _():
-        for part in range(3):
+        for part in range(2):
             sent(a_v.at[pl.ds(0, 8 * parts[part][1])], colp_s.at[part])
         sent(gx.at[pl.ds(0, 3)], g_s.at[0])
         sent(gz.at[pl.ds(0, 7)], g_s.at[1])
@@ -474,7 +503,7 @@
 
     @pl.when((r != 0) & (core == 0))
     def _():
-        for part in range(3):
+        for part in range(2):
             sent(colpb.at[pl.ds(*parts[part])], fwd_s.at[part])
 
     @pl.when(c == 0)
@@ -505,8 +534,7 @@
     high, low = split(right[...])
     columns = jnp.concatenate([high, low, high], axis=0)
     for t in range(6):
-        high, low = split(jnp.transpose(left[t]))
-        change = jnp.dot(jnp.concatenate([high, high, low], axis=1), columns, preferred_element_type=F32)
+        change = jnp.dot(left[t], columns, preferred_element_type=F32)
         for s in range(3):
             rows = pl.ds(t * 384 + s, 128, stride=3)
             tiles[rows, :] = a[rows, :] - change[:, 128 * s : 128 * s + 128]
@@ -530,14 +558,14 @@
     whole = pl.BlockSpec(memory_space=pltpu.VMEM)
     left, right = pl.pallas_call(
         kernel,
-        out_shape=[jax.ShapeDtypeStruct((6, 128, 128), F32), jax.ShapeDtypeStruct((128, 384), F32)],
+        out_shape=[jax.ShapeDtypeStruct((6, 128, 384), jnp.bfloat16), jax.ShapeDtypeStruct((128, 384), F32)],
         in_specs=[pl.BlockSpec(memory_space=pltpu.HBM)],
         out_specs=[whole, whole],
         scratch_shapes=[
             vmem(2304, 128), vmem(384, 128), vmem(2, 3, 128, 128), vmem(16, 3, 8, 128), vmem(32, 3, 8, 128),
             vmem(16, 3, 8, 128), vmem(8, 3, 8, 128), vmem(4, 32, 128), vmem(8, 32, 128), vmem(32, 128),
-            vmem(64, 128), vmem(1, 8, 128), vmem(16, 8, 128), vmem(16, 8, 128), vmem(128, 128), vmem(64, 128), vmem(64, 128),
-            dma(), dma(3), dma(3), dma(3), dma(), dma(), dma(3), dma(5), dma(), dma(), dma(2), dma(2), dma(), dma(),
+            vmem(64, 128), vmem(1, 8, 128), vmem(16, 8, 128), vmem(16, 8, 128), vmem(128, 128), vmem(64, 128), vmem(32, 128),
+            dma(), dma(2), dma(2), dma(2), dma(), dma(), dma(3), dma(5), dma(), dma(), dma(2), dma(2), dma(), dma(),
             dma(3), dma(3), dma(3), dma(), dma(), dma(), dma(), dma(), dma(2), dma(2),
         ],
         compiler_params=pltpu.CompilerParams(collective_id=0, has_side_effects=True, vmem_limit_bytes=54208 << 10),

time: 48.4 us -> 46.3 us (0.957)
  the two profiles are of different devices: /device:TPU:1 before, /device:TPU:64 now
where the time goes in v5:
time: 46.3 us; the launch traced here: 46.2 us
  Pallas kernels  46.2 us (100%)
    pallas_call x1, Pallas kernels, body(): pl.pallas_call(kernel, out_shape=[jax.ShapeDtypeStruct((6, 128, 384), jnp...  44.9 us
    pallas_call x1, Pallas kernels, body(): pl.pallas_call(update, out_shape=jax.ShapeDtypeStruct((2304, 128), F32),...  1.29 us

profile of v5, /device:TPU:64, one launch (start us, length us, event | category | flops | bytes accessed | tf_op | source)
XLA Modules:
  0.0 46.2 jit_solution(11543913793673536166)
XLA Ops:
  0.0 0.0 copy-start
  0.0 44.9 %panel.1 = (bf16[6,128,384]{2,1,0:T(8,128)(2,1)S(1)}, f32[128,384]{1,0:T(8,128)S(1)}) custom-call(f32[2304,128]{1,0:T(8,128)} %bitcast.2), custom_call_target="tpu_custom_call" | custom-call | tf_op jit(solution)/shard_map/panel/pallas_call | solution.py:559
  44.9 0.0 copy-done
  44.9 1.3 %update.1 = f32[2304,128]{1,0:T(8,128)} custom-call(f32[2304,128]{1,0:T(8,128)S(1)} %bitcast.3, bf16[6,128,384]{2,1,0:T(8,128)(2,1)S(1)} %get-tuple-element.7.left, f32[128,384]{1,0:T(8,128)S(1)} %get-tuple-element.8.right), custom_call_target="tpu_custom_call" | custom-call | tf_op jit(solution)/shard_map/update/pallas_call | solution.py:574
Async XLA Ops:
  0.0 44.9 %copy-start = (f32[6,1,128,3,1,128]{5,4,3,2,1,0:T(1,128)S(1)}, f32[6,1,128,3,1,128]{5,4,3,2,1,0:T(1,128)}, u32[]{:S(2)}) copy-start(f32[6,1,128,3,1,128]{5,4,3,2,1,0:T(1,128)} %param.1) | copy-start | bytes 3538948

commit v6 on v5

--- a/solution.py
+++ b/solution.py
@@ -111,7 +111,7 @@
 def kernel(
     a_hbm, left_o, right_o, a_v, colpb, rowpb, zpart, zrecv, zrows, zcols, gx, gz, gfin, p1, hsend, hrecv, hall, ct, c0, om,
     load_s, colp_s, colp_r, fwd_s, sc_s, sc_r, ag_s, ag_r, rs_s, rs_r, zr_s, zr_r, zc_s, zc_r,
-    g_s, g_r, p1_s, p1_r, h_s, h_r, ha_s, ha_r, c0_s, c0_r,
+    g_s, g_r, p1_s, p1_r, h_s, h_r, ha_s, ha_r,
 ):
     r, c = lax.axis_index("row"), lax.axis_index("col")
     y, core = lax.div(r, 2), lax.rem(r, 2)
@@ -140,6 +140,9 @@
     def x_peer(p):
         return z * 4 + lax.rem(x + spiral(p, 4), 4)
 
+    def far_peer(p):
+        return lax.rem(z + spiral(p, 8), 8) * 4 + lax.rem(x + 2, 4)
+
     def z_peer(p):
         return lax.rem(z + spiral(p, 8), 8) * 4 + x
 
@@ -176,7 +179,7 @@
 
     loop(0, 15, lambda p: greet((row_peer(p), c)))
 
-    @pl.when(jnp.logical_not(home))
+    @pl.when(jnp.logical_not(home) & (core == 0))
     def _():
         loop(0, 8, lambda g: greet((lax.rem(c, 16), panel_owner(g + 8 * lax.div(c, 16)))))
 
@@ -209,32 +212,26 @@
         def _():
             p1[...] = a_v[pl.ds(3 * NB, NB, stride=3), :]
 
-        colpb[...] = a_v[0:384, :]
-
-    when(owner, lambda: pl.semaphore_wait(barrier, 61))
+        colpb[...] = a_v[0:192, :]
+
+    when(owner & (core == 0), lambda: pl.semaphore_wait(barrier, 53))
+    when(owner & (core == 1), lambda: pl.semaphore_wait(barrier, 54))
     when(plain, lambda: pl.semaphore_wait(barrier, 46))
 
-    parts = ((0, 192), (192, 192))
-
-    def send_col(part):
-        rows = pl.ds(*parts[part])
-
-        def to(q):
-            other = 2 * spiral(q, 8) + jnp.where(q == 7, 1, 0)
-            copy(a_v.at[rows], colpb.at[rows], colp_s.at[part], colp_r.at[part], (other, c)).start()
-
-        loop(0, 8, to)
-
-    def wait_col(part):
-        rows = pl.ds(*parts[part])
-
+    columns = pl.ds(0, 192)
+
+    def send_col(q):
+        other = 2 * spiral(q, 8) + jnp.where(q == 7, 1, 0)
+        copy(a_v.at[columns], colpb, colp_s, colp_r, (other, c)).start()
+
+    def wait_col():
         @pl.when(r != 0)
         def _():
-            arrived(colpb.at[rows], colp_r.at[part])
+            arrived(colpb, colp_r)
 
             @pl.when(core == 0)
             def _():
-                copy(colpb.at[rows], colpb.at[rows], fwd_s.at[part], colp_r.at[part], (r + 1, c)).start()
+                copy(colpb, colpb, fwd_s.at[0], colp_r, (r + 1, c)).start()
 
     def scatter(part):
         def to(p):
@@ -248,7 +245,7 @@
 
     @pl.when(r == 0)
     def _():
-        send_col(0)
+        loop(0, 8, send_col)
         loop(0, 3, lambda p: copy(gx.at[x], gx.at[x], g_s.at[0], g_r.at[0], (r, x_peer(p))).start())
 
         @pl.when(c == 0)
@@ -257,7 +254,7 @@
 
     when(c == 0, lambda: scatter(1))
 
-    wait_col(0)
+    wait_col()
 
     def pass_to(k, part, dev, ssem, sem):
         copy(chunk(k, part), chunk(k, part), ag_s.at[ssem], ag_r.at[sem], (r, dev)).start()
@@ -274,7 +271,7 @@
         dev = z_peer(p)
         dev_z = lax.div(dev, 4)
         first = (lax.rem(dev_z + x, 2) == 0) & (lax.div(dev_z, 4) == my_h)
-        downs.append((dev, owner & (dev != 0) & jnp.logical_not(first), plain & (dev != 0)))
+        downs.append((dev, owner & (dev != 0) & jnp.logical_not(first)))
     acrosses = []
     for p in range(3):
         dev = x_peer(p)
@@ -282,8 +279,7 @@
         for i in range(4):
             k = 4 * i + 2 * lax.rem(x, 2) + lax.div(x, 2)
             skip = dev_owner & (lax.div(z, 4) == i // 2)
-            k_b = 4 * i + 2 * lax.rem(x + 1, 2) + lax.div(x, 2)
-            acrosses.append((dev, k, (dev != 0) & jnp.logical_not(skip), k_b, dev != 0))
+            acrosses.append((dev, k, (dev != 0) & jnp.logical_not(skip)))
 
     panel = jnp.concatenate([panel_cols(colpb, s) for s in range(3)], axis=1)
     def share(t):
@@ -319,40 +315,38 @@
     for dev, go in firsts:
         when(go, functools.partial(pass_to, mine, 0, dev, 0, 2))
         n_first = n_first + jnp.where(go, one, 0)
-    loop(0, 8, reduce_to)
+    loop(0, 8, lambda p: reduce_to(7 - p))
     for t in (1, 3, 5):
         share(t)
     loop(8, 16, reduce_to)
 
-    when(r == 0, lambda: send_col(1))
-
-    for dev, go, go_b in downs:
+    for dev, go in downs:
         when(go, functools.partial(pass_to, mine, 0, dev, 0, 0))
         n_first = n_first + jnp.where(go, one, 0)
 
-    for dev, k, go, k_b, go_b in acrosses:
+    for dev, k, go in acrosses:
         n_across = n_across + jnp.where(go, one, 0)
-        n_b = n_b + jnp.where(go_b, one, 0)
+
+    when(plain, lambda: arrived(chunk(mine, 1), sc_r))
+    for p in range(8):
+        dev = panel_owner(8 * my_h + lax.rem(my_g + 4 + p, 8))
+        when(plain & (dev != 0), functools.partial(pass_to, mine, 1, dev, 2, 1))
+        n_b = n_b + jnp.where(plain & (dev != 0), one, 0)
 
     def pass_across():
-        for dev, k, go, k_b, go_b in acrosses:
+        for dev, k, go in acrosses:
             when(go, functools.partial(pass_to, k, 0, dev, 1, 3))
-        for dev, k, go, k_b, go_b in acrosses:
-            when(go_b, functools.partial(pass_to, k_b, 1, dev, 2, 4))
 
     def z_across():
         def to(p):
             k = 4 * lax.rem(p, 4) + 2 * lax.rem(x, 2) + lax.div(x, 2)
-            copy(zrows.at[k], zrows.at[k], zr_s.at[1], zr_r.at[1], (r, x_peer(lax.div(p, 4)))).start()
-
-        loop(0, 12, to)
+            copy(zrows.at[k], zrows.at[k], zr_s.at[1], zr_r.at[1], (r, x_peer(1 + lax.div(p, 4)))).start()
+
+        loop(0, 8, to)
 
     def sent_some(n, sem, least, most):
         for count in range(least, most + 1):
             when(n == count, lambda count=count: sent(some(count), sem))
-
-    for dev, go, go_b in downs:
-        n_b = n_b + jnp.where(go_b, one, 0)
 
     @pl.when(r == 0)
     def _():
@@ -363,33 +357,62 @@
         loop(0, 15, lambda p: copy(p1, p1, p1_s.at[2], p1_r, (row_peer(p), c)).start())
 
 
+    def gram_matrix():
+        packed = gfin[...]
+        gram = jnp.concatenate([packed, pltpu.roll(packed, 64, 1)], axis=0)
+        return jnp.where(lane < NB, gram, 0.0)
+
+    def cholesky():
+        when(r != 0, lambda: arrived(gfin, g_r.at[2]))
+        ct[0:NB, :] = jnp.zeros((NB, 128), F32)
+        factor_cholesky(gram_matrix(), ct)
+        c0[...] = jnp.transpose(ct[...])[0:NB, :]
+
+    def inverse():
+        when(r != 0, lambda: arrived(p1, p1_r))
+        corner = p1[...]
+        product = dot_nn(pltpu.roll(c0[...], 64, 1), jnp.concatenate([corner, jnp.zeros_like(corner)], axis=0))
+        whole = invert(gram_matrix() + jnp.where(lane < NB, product, 0.0))
+        om[...] = whole
+
     @pl.when(owner)
     def _():
+        cholesky()
+        when(c != 0, lambda: arrived(some(7), ag_r.at[2]))
+        rows = jnp.concatenate([rowpb[my_h, i, 0:NB, :] for i in range(3)], axis=1)
+        high, low = split(jnp.concatenate([rows, jnp.zeros_like(rows)], axis=0))
         arrived(some(31), rs_r)
         zrecv[c] = zpart[mine]
         zsum = lax.fori_loop(1, 32, lambda i, total: total + zrecv[i], zrecv[0])
-        zrows[mine] = zsum
-        when(c != 0, lambda: arrived(some(7), ag_r.at[2]))
-        rows = jnp.concatenate([rowpb[my_h, i, 0:NB, :] for i in range(3)], axis=1)
-        total = dot3(
-            jnp.concatenate([zsum[i] for i in range(3)], axis=1),
-            jnp.concatenate([rows, jnp.zeros_like(rows)], axis=0),
-            (1, 1),
+        z_rows = jnp.concatenate([zsum[i] for i in range(3)], axis=1)
+        z_high, z_low = split(z_rows)
+        total = lax.dot_general(
+            jnp.concatenate([z_high, z_high, z_low], axis=1),
+            jnp.concatenate([high, low, high], axis=1),
+            (((1,), (1,)), ((), ())),
+            preferred_element_type=F32,
         )
         lane8 = lax.broadcasted_iota(jnp.int32, (8, 128), 1)
         total = total + jnp.where((r == 0) & (my_h == 0) & (lane8 >= NB), zsum[0], 0.0)
         hsend[0] = total
         hrecv[r] = total
         loop(0, 15, lambda p: copy(hsend.at[0], hrecv.at[r], h_s, h_r, (row_peer(p), c)).start())
+        when(c != 0, lambda: arrived(some(8), ag_r.at[1]))
+        mine_c = c0[pl.ds(pl.multiple_of(8 * my_g, 8), 8), :]
+        y_rows = z_rows + dot3(mine_c, jnp.concatenate([rowpb[my_h, i] for i in range(3)], axis=1), (1, 0))
+        for i in range(3):
+            zrows[mine, i] = y_rows[:, 128 * i : 128 * i + 128]
         there = r + 16 * my_h
-        loop(0, 15, lambda p: copy(zrows.at[mine], zcols.at[my_g], zc_s, zc_r, (row_peer(p), there)).start())
+
         loop(0, 7, lambda p: copy(zrows.at[mine], zrows.at[mine], zr_s.at[0], zr_r.at[0], (r, z_peer(p))).start())
-        wait_col(1)
-        @pl.when(c != 0)
-        def _():
-            arrived(some(2), ag_r.at[0])
-            arrived(some(4), ag_r.at[1])
-
+        loop(0, 8, lambda p: copy(zrows.at[mine], zrows.at[mine], zr_s.at[0], zr_r.at[2], (r, far_peer(p))).start())
+        def to_cols(p):
+            dev = 2 * lax.rem(y + spiral(p, 8), 8)
+            when(dev != r, lambda: copy(zrows.at[mine], zcols.at[my_g], zc_s, zc_r, (dev, there)).start())
+
+        loop(0, 8, to_cols)
+        inverse()
+        when(c != 0, lambda: arrived(some(2), ag_r.at[0]))
         pass_across()
         arrived(hrecv.at[pl.ds(0, 15)], h_r)
         hall[mine] = lax.fori_loop(1, 16, lambda i, total: total + hrecv[i], hrecv[0])
@@ -399,67 +422,53 @@
         @pl.when(c != 0)
         def _():
             arrived(some(6), ag_r.at[3])
-            arrived(some(12), ag_r.at[4])
-
-        @pl.when(r != 0)
-        def _():
-            arrived(gfin, g_r.at[2])
-            arrived(p1, p1_r)
-
-        arrived(c0, c0_r.at[0])
-        arrived(om, c0_r.at[1])
+
 
     @pl.when(plain)
     def _():
-        when(r != 0, lambda: arrived(gfin, g_r.at[2]))
-        arrived(chunk(mine, 1), sc_r)
-        for dev, go, go_b in downs:
-            when(go_b, functools.partial(pass_to, mine, 1, dev, 2, 1))
-        packed = gfin[...]
-        gram = jnp.concatenate([packed, pltpu.roll(packed, 64, 1)], axis=0)
-        gram = jnp.where(lane < NB, gram, 0.0)
-        ct[0:NB, :] = jnp.zeros((NB, 128), F32)
-        factor_cholesky(gram, ct)
-        c0[...] = jnp.transpose(ct[...])[0:NB, :]
-        copy(c0, c0, c0_s.at[0], c0_r.at[0], (r, partner)).start()
-        when(r != 0, lambda: arrived(p1, p1_r))
-        corner = p1[...]
-        product = dot_nn(pltpu.roll(c0[...], 64, 1), jnp.concatenate([corner, jnp.zeros_like(corner)], axis=0))
-        whole = invert(gram + jnp.where(lane < NB, product, 0.0))
-        om[...] = whole[0:32, :] + pltpu.roll(whole[32:, :], 64, 1)
-        copy(om, om, c0_s.at[1], c0_r.at[1], (r, partner)).start()
-        wait_col(1)
+        cholesky()
+        inverse()
         arrived(some(4), ag_r.at[0])
-        arrived(some(3), ag_r.at[1])
         pass_across()
         arrived(some(4), zr_r.at[0])
         z_across()
         arrived(some(12), ag_r.at[3])
-        arrived(some(12), ag_r.at[4])
-
+
+    def forward_cols():
+        copy(zcols, zcols, fwd_s.at[1], zc_r, (r + 1, c)).start()
+
+    home_next = lax.rem(c, 16) == r + 1
+
+    @pl.when(jnp.logical_not(home) & (core == 0))
+    def _():
+        arrived(zcols, zc_r)
+        when(jnp.logical_not(home_next), forward_cols)
+
+    inverse_t = om[:, 0:NB]
+    pad = jnp.zeros((NB, 128), F32)
     sub = lax.broadcasted_iota(jnp.int32, (NB, 128), 0)
-    c0v = c0[...]
     unit = jnp.where(sub == lane, 1.0, 0.0)
-    pad = jnp.zeros((NB, 128), F32)
-    packed_om = om[...]
-    inverse = jnp.where(lane < NB, jnp.concatenate([packed_om, pltpu.roll(packed_om, 64, 1)], axis=0), 0.0)
-    s_mat = dot_nn(inverse, jnp.concatenate([unit + c0v, pad], axis=0))
-    c_cols = jnp.where(c == 0, c0v, 0.0)
-    c_rows = jnp.where(r == 0, c0v, 0.0)
-
-    arrived(some(12), zr_r.at[1])
-
-    zb, n_rows = [], []
+    s_mat = dot_nn(inverse_t, unit + c0[...])
+    turned = jnp.transpose(jnp.concatenate([s_mat, pad], axis=0))
+    c_cols = jnp.where(c == 0, c0[...], 0.0)
+    c_rows = jnp.where(r == 0, c0[...], 0.0)
+    n_cols = [panel_cols(colpb, s) for s in range(3)]
+    n_cols = jnp.concatenate([n_cols[0] + c_cols] + n_cols[1:], axis=1)
+    right_o[0:NB, :] = n_cols
+    sn_cols = dot3(turned[:, 0:NB], n_cols, (1, 0))
+
+    arrived(some(4), zr_r.at[2])
+    arrived(some(8), zr_r.at[1])
+
+    y_rows, n_rows = [], []
     for t in range(6):
         h, i = t % 2, t // 2
-        zb.append(
-            jnp.concatenate([zrows[8 * h : 8 * h + 8, i].reshape(NB, 128), rowpb[h, i, NB:, :]], axis=0)
-        )
+        y_rows.append(zrows[8 * h : 8 * h + 8, i].reshape(NB, 128))
         n_t = rowpb[h, i, 0:NB, :]
         if t == 0:
             n_t = n_t + c_rows
         n_rows.append(n_t)
-    w_rows = dot3(s_mat, jnp.concatenate(zb, axis=1), (1, 0))
+    w_rows = dot3(inverse_t, jnp.concatenate(y_rows, axis=1), (1, 0))
     for t in range(6):
         rows = jnp.concatenate([w_rows[:, 128 * t : 128 * t + 128], n_rows[t]], axis=0)
         high, low = split(jnp.transpose(rows))
@@ -469,17 +478,11 @@
     def _():
         zcols[...] = zrows[pl.ds(8 * lax.div(c, 16), 8)]
 
-    when(jnp.logical_not(home), lambda: arrived(zcols, zc_r))
-
-    zb = [
-        jnp.concatenate([zcols[:, s].reshape(NB, 128), colpb[pl.ds(192 + s, NB, stride=3), :]], axis=0) for s in range(3)
-    ]
-    w_cols = dot3(s_mat, jnp.concatenate(zb, axis=1), (1, 0))
-    n_cols = [panel_cols(colpb, s) for s in range(3)]
-    n_cols = jnp.concatenate([n_cols[0] + c_cols] + n_cols[1:], axis=1)
-    right_o[0:NB, :] = n_cols
-    s_turned = jnp.transpose(jnp.concatenate([s_mat, pad], axis=0))
-    sn_cols = dot3(s_turned[:, 0:NB], n_cols, (1, 0))
+    when(home & (core == 0), forward_cols)
+    when(jnp.logical_not(home) & (core == 1), lambda: arrived(zcols, zc_r))
+
+    y_cols = jnp.concatenate([zcols[:, s].reshape(NB, 128) for s in range(3)], axis=1)
+    w_cols = dot3(inverse_t, y_cols, (1, 0))
 
     when(owner, lambda: arrived(hall.at[pl.ds(0, 15)], ha_r))
     when(plain, lambda: arrived(hall, ha_r))
@@ -492,8 +495,7 @@
 
     @pl.when(r == 0)
     def _():
-        for part in range(2):
-            sent(a_v.at[pl.ds(0, 8 * parts[part][1])], colp_s.at[part])
+        sent(a_v.at[pl.ds(0, 8 * 192)], colp_s)
         sent(gx.at[pl.ds(0, 3)], g_s.at[0])
         sent(gz.at[pl.ds(0, 7)], g_s.at[1])
         sent(a_v.at[pl.ds(0, 15 * 32)], g_s.at[2])
@@ -503,8 +505,7 @@
 
     @pl.when((r != 0) & (core == 0))
     def _():
-        for part in range(2):
-            sent(colpb.at[pl.ds(*parts[part])], fwd_s.at[part])
+        sent(colpb, fwd_s.at[0])
 
     @pl.when(c == 0)
     def _():
@@ -512,22 +513,23 @@
 
     when(owner, lambda: sent_some(n_first, ag_s.at[0], 10, 14))
     sent_some(n_across, ag_s.at[1], 4, 12)
-    sent(some(12), zr_s.at[1])
-    sent_some(n_b, ag_s.at[2], 8, 19)
+    sent(some(8), zr_s.at[1])
+    when(plain, lambda: sent_some(n_b, ag_s.at[2], 7, 8))
 
     @pl.when(owner)
     def _():
         sent(some(15), rs_s)
-        sent(some(15), zc_s)
-        sent(some(7), zr_s.at[0])
+        when(core == 0, lambda: sent(some(7), zc_s))
+        when(core == 1, lambda: sent(some(8), zc_s))
+        sent(some(15), zr_s.at[0])
         sent(a_v.at[pl.ds(0, 15 * 8)], h_s)
         sent(a_v.at[pl.ds(0, 31 * 8)], ha_s)
 
+    when((core == 0) & jnp.logical_not(home_next), lambda: sent(zcols, fwd_s.at[1]))
+
     @pl.when(plain)
     def _():
         sent(some(16), rs_s)
-        sent(c0, c0_s.at[0])
-        sent(om, c0_s.at[1])
 
 
 def update(a, left, right, out, tiles, sems):
@@ -562,11 +564,11 @@
         in_specs=[pl.BlockSpec(memory_space=pltpu.HBM)],
         out_specs=[whole, whole],
         scratch_shapes=[
-            vmem(2304, 128), vmem(384, 128), vmem(2, 3, 128, 128), vmem(16, 3, 8, 128), vmem(32, 3, 8, 128),
+            vmem(2304, 128), vmem(192, 128), vmem(2, 3, 128, 128), vmem(16, 3, 8, 128), vmem(32, 3, 8, 128),
             vmem(16, 3, 8, 128), vmem(8, 3, 8, 128), vmem(4, 32, 128), vmem(8, 32, 128), vmem(32, 128),
-            vmem(64, 128), vmem(1, 8, 128), vmem(16, 8, 128), vmem(16, 8, 128), vmem(128, 128), vmem(64, 128), vmem(32, 128),
-            dma(), dma(2), dma(2), dma(2), dma(), dma(), dma(3), dma(5), dma(), dma(), dma(2), dma(2), dma(), dma(),
-            dma(3), dma(3), dma(3), dma(), dma(), dma(), dma(), dma(), dma(2), dma(2),
+            vmem(64, 128), vmem(1, 8, 128), vmem(16, 8, 128), vmem(16, 8, 128), vmem(128, 128), vmem(64, 128), vmem(64, 128),
+            dma(), dma(), dma(), dma(2), dma(), dma(), dma(3), dma(4), dma(), dma(), dma(2), dma(3), dma(), dma(),
+            dma(3), dma(3), dma(3), dma(), dma(), dma(), dma(), dma(),
         ],
         compiler_params=pltpu.CompilerParams(collective_id=0, has_side_effects=True, vmem_limit_bytes=54208 << 10),
         name="panel",

time: 46.3 us -> 45.4 us (0.981)
  the two profiles are of different devices: /device:TPU:64 before, /device:TPU:1 now
where the time goes in v6:
time: 45.4 us; the launch traced here: 45.3 us
  Pallas kernels  45.3 us (100%)
    pallas_call x1, Pallas kernels, body(): pl.pallas_call(kernel, out_shape=[jax.ShapeDtypeStruct((6, 128, 384), jnp...  44 us
    pallas_call x1, Pallas kernels, body(): pl.pallas_call(update, out_shape=jax.ShapeDtypeStruct((2304, 128), F32),...  1.29 us

profile of v6, /device:TPU:1, one launch (start us, length us, event | category | flops | bytes accessed | tf_op | source)
XLA Modules:
  0.0 45.3 jit_solution(15852613828508716896)
XLA Ops:
  0.0 0.0 copy-start
  0.0 44.0 %panel.1 = (bf16[6,128,384]{2,1,0:T(8,128)(2,1)S(1)}, f32[128,384]{1,0:T(8,128)S(1)}) custom-call(f32[2304,128]{1,0:T(8,128)} %bitcast.2), custom_call_target="tpu_custom_call" | custom-call | tf_op jit(solution)/shard_map/panel/pallas_call | solution.py:561
  44.0 0.0 copy-done
  44.0 1.3 %update.1 = f32[2304,128]{1,0:T(8,128)} custom-call(f32[2304,128]{1,0:T(8,128)S(1)} %bitcast.3, bf16[6,128,384]{2,1,0:T(8,128)(2,1)S(1)} %get-tuple-element.7.left, f32[128,384]{1,0:T(8,128)S(1)} %get-tuple-element.8.right), custom_call_target="tpu_custom_call" | custom-call | tf_op jit(solution)/shard_map/update/pallas_call | solution.py:576
Async XLA Ops:
  0.0 44.0 %copy-start = (f32[6,1,128,3,1,128]{5,4,3,2,1,0:T(1,128)S(1)}, f32[6,1,128,3,1,128]{5,4,3,2,1,0:T(1,128)}, u32[]{:S(2)}) copy-start(f32[6,1,128,3,1,128]{5,4,3,2,1,0:T(1,128)} %param.1) | copy-start | bytes 3538948

commit v7 on v6

--- a/solution.py
+++ b/solution.py
@@ -411,9 +411,9 @@
             when(dev != r, lambda: copy(zrows.at[mine], zcols.at[my_g], zc_s, zc_r, (dev, there)).start())
 
         loop(0, 8, to_cols)
-        inverse()
         when(c != 0, lambda: arrived(some(2), ag_r.at[0]))
         pass_across()
+        inverse()
         arrived(hrecv.at[pl.ds(0, 15)], h_r)
         hall[mine] = lax.fori_loop(1, 16, lambda i, total: total + hrecv[i], hrecv[0])
         loop(0, 31, lambda p: copy(hall.at[mine], hall.at[mine], ha_s, ha_r, (r, early_peer(p))).start())
@@ -426,10 +426,10 @@
 
     @pl.when(plain)
     def _():
+        arrived(some(4), ag_r.at[0])
+        pass_across()
         cholesky()
         inverse()
-        arrived(some(4), ag_r.at[0])
-        pass_across()
         arrived(some(4), zr_r.at[0])
         z_across()
         arrived(some(12), ag_r.at[3])

time: 45.4 us -> 45.4 us (level)
  no operation moved by 1% of the time
where the time goes in v7:
time: 45.4 us; the launch traced here: 45.3 us
  Pallas kernels  45.3 us (100%)
    pallas_call x1, Pallas kernels, body(): pl.pallas_call(kernel, out_shape=[jax.ShapeDtypeStruct((6, 128, 384), jnp...  44 us
    pallas_call x1, Pallas kernels, body(): pl.pallas_call(update, out_shape=jax.ShapeDtypeStruct((2304, 128), F32),...  1.29 us

profile of v7, /device:TPU:1, one launch (start us, length us, event | category | flops | bytes accessed | tf_op | source)
XLA Modules:
  0.0 45.3 jit_solution(6918739557764717592)
XLA Ops:
  0.0 0.0 copy-start
  0.0 44.0 %panel.1 = (bf16[6,128,384]{2,1,0:T(8,128)(2,1)S(1)}, f32[128,384]{1,0:T(8,128)S(1)}) custom-call(f32[2304,128]{1,0:T(8,128)} %bitcast.2), custom_call_target="tpu_custom_call" | custom-call | tf_op jit(solution)/shard_map/panel/pallas_call | solution.py:561
  44.0 0.0 copy-done
  44.0 1.3 %update.1 = f32[2304,128]{1,0:T(8,128)} custom-call(f32[2304,128]{1,0:T(8,128)S(1)} %bitcast.3, bf16[6,128,384]{2,1,0:T(8,128)(2,1)S(1)} %get-tuple-element.7.left, f32[128,384]{1,0:T(8,128)S(1)} %get-tuple-element.8.right), custom_call_target="tpu_custom_call" | custom-call | tf_op jit(solution)/shard_map/update/pallas_call | solution.py:576
Async XLA Ops:
  0.0 44.0 %copy-start = (f32[6,1,128,3,1,128]{5,4,3,2,1,0:T(1,128)S(1)}, f32[6,1,128,3,1,128]{5,4,3,2,1,0:T(1,128)}, u32[]{:S(2)}) copy-start(f32[6,1,128,3,1,128]{5,4,3,2,1,0:T(1,128)} %param.1) | copy-start | bytes 3538948

commit v8 on v7

--- a/solution.py
+++ b/solution.py
@@ -59,6 +59,12 @@
 
 def spiral(q, n):
     return lax.rem(n // 2 + (1 - 2 * lax.rem(q, 2)) * lax.div(q + 1, 2), n)
+
+
+def tree_sum(terms):
+    while len(terms) > 1:
+        terms = [a + b for a, b in zip(terms[0::2], terms[1::2])]
+    return terms[0]
 
 
 def loop(lo, hi, f):
@@ -383,7 +389,7 @@
         high, low = split(jnp.concatenate([rows, jnp.zeros_like(rows)], axis=0))
         arrived(some(31), rs_r)
         zrecv[c] = zpart[mine]
-        zsum = lax.fori_loop(1, 32, lambda i, total: total + zrecv[i], zrecv[0])
+        zsum = tree_sum([zrecv[i] for i in range(32)])
         z_rows = jnp.concatenate([zsum[i] for i in range(3)], axis=1)
         z_high, z_low = split(z_rows)
         total = lax.dot_general(
@@ -415,7 +421,7 @@
         pass_across()
         inverse()
         arrived(hrecv.at[pl.ds(0, 15)], h_r)
-        hall[mine] = lax.fori_loop(1, 16, lambda i, total: total + hrecv[i], hrecv[0])
+        hall[mine] = tree_sum([hrecv[i] for i in range(16)])
         loop(0, 31, lambda p: copy(hall.at[mine], hall.at[mine], ha_s, ha_r, (r, early_peer(p))).start())
         arrived(some(3), zr_r.at[0])
         z_across()

time: 45.4 us -> 45.3 us (level)
  no operation moved by 1% of the time
where the time goes in v8:
time: 45.3 us; the launch traced here: 45.2 us
  Pallas kernels  45.2 us (100%)
    pallas_call x1, Pallas kernels, body(): pl.pallas_call(kernel, out_shape=[jax.ShapeDtypeStruct((6, 128, 384), jnp...  43.9 us
    pallas_call x1, Pallas kernels, body(): pl.pallas_call(update, out_shape=jax.ShapeDtypeStruct((2304, 128), F32),...  1.29 us

profile of v8, /device:TPU:1, one launch (start us, length us, event | category | flops | bytes accessed | tf_op | source)
XLA Modules:
  0.0 45.2 jit_solution(18024005144868313037)
XLA Ops:
  0.0 0.0 copy-start
  0.0 43.9 %panel.1 = (bf16[6,128,384]{2,1,0:T(8,128)(2,1)S(1)}, f32[128,384]{1,0:T(8,128)S(1)}) custom-call(f32[2304,128]{1,0:T(8,128)} %bitcast.2), custom_call_target="tpu_custom_call" | custom-call | tf_op jit(solution)/shard_map/panel/pallas_call | solution.py:567
  43.9 0.0 copy-done
  43.9 1.3 %update.1 = f32[2304,128]{1,0:T(8,128)} custom-call(f32[2304,128]{1,0:T(8,128)S(1)} %bitcast.3, bf16[6,128,384]{2,1,0:T(8,128)(2,1)S(1)} %get-tuple-element.7.left, f32[128,384]{1,0:T(8,128)S(1)} %get-tuple-element.8.right), custom_call_target="tpu_custom_call" | custom-call | tf_op jit(solution)/shard_map/update/pallas_call | solution.py:582
Async XLA Ops:
  0.0 43.9 %copy-start = (f32[6,1,128,3,1,128]{5,4,3,2,1,0:T(1,128)S(1)}, f32[6,1,128,3,1,128]{5,4,3,2,1,0:T(1,128)}, u32[]{:S(2)}) copy-start(f32[6,1,128,3,1,128]{5,4,3,2,1,0:T(1,128)} %param.1) | copy-start | bytes 3538948

commit v9 on v8

--- a/solution.py
+++ b/solution.py
@@ -461,7 +461,10 @@
     n_cols = [panel_cols(colpb, s) for s in range(3)]
     n_cols = jnp.concatenate([n_cols[0] + c_cols] + n_cols[1:], axis=1)
     right_o[0:NB, :] = n_cols
-    sn_cols = dot3(turned[:, 0:NB], n_cols, (1, 0))
+    sn_high, sn_low = split(dot3(turned[:, 0:NB], n_cols, (1, 0)))
+    sn_cols = jnp.concatenate([sn_high, sn_low, sn_high], axis=0)
+    s_high, s_low = split(s_mat)
+    s_left = jnp.concatenate([s_high, s_high, s_low], axis=1)
 
     arrived(some(4), zr_r.at[2])
     arrived(some(8), zr_r.at[1])
@@ -496,8 +499,11 @@
     top = (hall[0:8] + hall[8:16]).reshape(NB, 128)
     turned = jnp.transpose(jnp.concatenate([top, pad], axis=0))
     bottom = jnp.where(lane < NB, turned[NB:, :], p1[...])
-    inner = dot3(jnp.concatenate([top, bottom], axis=0), sn_cols, (1, 0))
-    right_o[NB:, :] = w_cols - dot3(s_mat, inner, (1, 0))
+    m_high, m_low = split(jnp.concatenate([top, bottom], axis=0))
+    m_left = jnp.concatenate([m_high, m_high, m_low], axis=1)
+    high, low = split(jnp.dot(m_left, sn_cols, preferred_element_type=F32))
+    inner = jnp.concatenate([high, low, high], axis=0)
+    right_o[NB:, :] = w_cols - jnp.dot(s_left, inner, preferred_element_type=F32)
 
     @pl.when(r == 0)
     def _():

time: 45.3 us -> 45.3 us (level)
  no operation moved by 1% of the time
where the time goes in v9:
time: 45.3 us; the launch traced here: 45.2 us
  Pallas kernels  45.2 us (100%)
    pallas_call x1, Pallas kernels, body(): pl.pallas_call(kernel, out_shape=[jax.ShapeDtypeStruct((6, 128, 384), jnp...  43.9 us
    pallas_call x1, Pallas kernels, body(): pl.pallas_call(update, out_shape=jax.ShapeDtypeStruct((2304, 128), F32),...  1.29 us

profile of v9, /device:TPU:1, one launch (start us, length us, event | category | flops | bytes accessed | tf_op | source)
XLA Modules:
  0.0 45.2 jit_solution(3366791114734273315)
XLA Ops:
  0.0 0.0 copy-start
  0.0 43.9 %panel.1 = (bf16[6,128,384]{2,1,0:T(8,128)(2,1)S(1)}, f32[128,384]{1,0:T(8,128)S(1)}) custom-call(f32[2304,128]{1,0:T(8,128)} %bitcast.2), custom_call_target="tpu_custom_call" | custom-call | tf_op jit(solution)/shard_map/panel/pallas_call | solution.py:573
  43.9 0.0 copy-done
  43.9 1.3 %update.1 = f32[2304,128]{1,0:T(8,128)} custom-call(f32[2304,128]{1,0:T(8,128)S(1)} %bitcast.3, bf16[6,128,384]{2,1,0:T(8,128)(2,1)S(1)} %get-tuple-element.7.left, f32[128,384]{1,0:T(8,128)S(1)} %get-tuple-element.8.right), custom_call_target="tpu_custom_call" | custom-call | tf_op jit(solution)/shard_map/update/pallas_call | solution.py:588
Async XLA Ops:
  0.0 43.9 %copy-start = (f32[6,1,128,3,1,128]{5,4,3,2,1,0:T(1,128)S(1)}, f32[6,1,128,3,1,128]{5,4,3,2,1,0:T(1,128)}, u32[]{:S(2)}) copy-start(f32[6,1,128,3,1,128]{5,4,3,2,1,0:T(1,128)} %param.1) | copy-start | bytes 3538948
